TPU v7x, 256 devices: a whole 4x4x8 slice. The times are simulated.
256 devices in a mesh: feat: 4 (over x), graph: 16 (over z, core), dp: 4 (over y).
Axes of the slice: x: 4, y: 4, z: 8, core: 2. Of those that a mesh axis runs over, the one named last changes fastest.
Arguments:
- features: bfloat16 [4, 32768, 768], P('dp', 'graph', 'feat'), may hold values from -6 to 6
- w1_self: bfloat16 [768, 1024], P('feat'), may hold values from -0.21875 to 0.21875
- w1_neigh: bfloat16 [768, 1024], P('feat'), may hold values from -0.625 to 0.625
- w2_self: bfloat16 [1024, 153], P('feat'), may hold values from -0.1875 to 0.1875
- w2_neigh: bfloat16 [1024, 153], P('feat'), may hold values from -0.5 to 0.5
- tile_rows: int32 [4, 16, 16, 3], P('dp', 'graph'), may hold values from 0 to 11, as said below
- tile_cols: int32 [4, 16, 16, 3], P('dp', 'graph'), may hold values from 0 to 15, as said below
- tile_count: int32 [4, 16, 16], P('dp', 'graph'), may hold values from 0 to 3, as said below
- tile_bits: int32 [4, 16, 16, 3, 128, 128], P('dp', 'graph'), may hold values 0 or 1
- d_logits: bfloat16 [4, 32768, 153], P('dp', 'graph'), may hold values from -0.119628906 to 0.119628906
Outputs:
- logits: float32 [4, 32768, 153], P('dp', 'graph')
- g_w1_self: float32 [768, 1024], P('feat')
- g_w1_neigh: float32 [768, 1024], P('feat')
- g_w2_self: float32 [1024, 153], P('feat')
- g_w2_neigh: float32 [1024, 153], P('feat')
Inputs may be any that keep to these rules, and one draw needn't show every extreme that they name: `tile_rows`: row blocks 3 * 4 and above of every partition hold frontier nodes and are named by no slot. `tile_cols`: the column blocks of the 3 slots of one partition and one owner are distinct, dead slots included. `tile_count`: in every minibatch some owner has 3 live slots in every partition.
All inputs are finite; a program needn't handle non-finite values. No bound on the sum of `tile_bits` on one device may be relied on, other than what follows from the above.
Results may differ from a plain program's by a relative error of at most 0.0045.
Values may be sent and summed in bfloat16 or wider, within the bound.
A program may use at most 128 MiB of HBM per device.

v0:
```python
import jax
import jax.numpy as jnp
from jax import lax
from jax.sharding import PartitionSpec as P

TILE = 128


highest = lax.Precision.HIGHEST


def on_device(
    features,
    w1_self,
    w1_neigh,
    w2_self,
    w2_neigh,
    tile_rows,
    tile_cols,
    tile_count,
    tile_bits,
    d_logits,
):
    own_feats = features[0]
    slot_rows = tile_rows[0, 0]
    slot_cols = tile_cols[0, 0]
    slot_count = tile_count[0, 0]
    node_count = own_feats.shape[0]
    block_count = node_count // TILE
    n_slots = slot_rows.shape[0] * slot_rows.shape[1]
    is_live = jnp.arange(slot_rows.shape[1], dtype=jnp.int32)[None, :] < slot_count[:, None]
    live_bits = jnp.where(is_live[:, :, None, None], tile_bits[0, 0], 0)
    bits_low = live_bits.astype(jnp.bfloat16)
    block_ids = jnp.arange(block_count, dtype=jnp.int32)
    row_onehot = (
        ((slot_rows[None] == block_ids[:, None, None]) & is_live[None])
        .astype(jnp.float32)
        .reshape(block_count, n_slots)
    )
    row_totals = jnp.sum(live_bits, axis=3).astype(jnp.float32).reshape(n_slots, TILE)
    degree = jnp.dot(row_onehot, row_totals, precision=highest).reshape(node_count)
    inverse = (1.0 / jnp.maximum(degree, 1.0))[:, None]
    requested = lax.all_to_all(slot_cols, "graph", split_axis=0, concat_axis=0, tiled=True)
    col_onehot = (
        (requested[None] == block_ids[:, None, None])
        .astype(jnp.bfloat16)
        .reshape(block_count, n_slots)
    )

    def gather_rows(source):
        width = source.shape[1]
        picked = source.reshape(block_count, TILE, width)[requested]
        arrived = lax.all_to_all(picked, "graph", split_axis=0, concat_axis=0, tiled=True)
        terms = jnp.einsum("osij,osjw->osiw", bits_low, arrived, preferred_element_type=jnp.float32)
        summed = jnp.dot(row_onehot, terms.reshape(n_slots, TILE * width), precision=highest)
        return summed.reshape(node_count, width)

    neigh_feats = (inverse * gather_rows(own_feats)).astype(jnp.bfloat16)
    partial_sum = jnp.dot(own_feats, w1_self, preferred_element_type=jnp.float32) + jnp.dot(
        neigh_feats, w1_neigh, preferred_element_type=jnp.float32
    )
    pre_act = lax.psum_scatter(partial_sum, "feat", scatter_dimension=1, tiled=True)
    hidden = jax.nn.silu(pre_act).astype(jnp.bfloat16)
    neigh_mean = (inverse * gather_rows(hidden)).astype(jnp.bfloat16)
    partial_logits = jnp.dot(hidden, w2_self, preferred_element_type=jnp.float32) + jnp.dot(
        neigh_mean, w2_neigh, preferred_element_type=jnp.float32
    )
    logits = lax.psum(partial_logits, "feat")
    grad_out = d_logits[0]
    grad_second_self = jnp.dot(hidden.T, grad_out, preferred_element_type=jnp.float32)
    grad_second_neigh = jnp.dot(neigh_mean.T, grad_out, preferred_element_type=jnp.float32)
    scaled_two = (
        inverse * jnp.dot(grad_out, w2_neigh.T, preferred_element_type=jnp.float32)
    ).astype(jnp.bfloat16)
    width = scaled_two.shape[1]
    picked = scaled_two.reshape(block_count, TILE, width)[slot_rows]
    terms = jnp.einsum(
        "osij,osiw->osjw", bits_low, picked, preferred_element_type=jnp.float32
    ).astype(jnp.bfloat16)
    arrived = lax.all_to_all(terms, "graph", split_axis=0, concat_axis=0, tiled=True)
    summed = jnp.dot(
        col_onehot, arrived.reshape(n_slots, TILE * width), preferred_element_type=jnp.float32
    )
    grad_hidden = jnp.dot(grad_out, w2_self.T, preferred_element_type=jnp.float32) + summed.reshape(
        node_count, width
    )
    logistic = jax.nn.sigmoid(pre_act)
    grad_pre_low = (grad_hidden * logistic * (1.0 + pre_act * (1.0 - logistic))).astype(
        jnp.bfloat16
    )
    layer_inputs = jnp.stack([own_feats, neigh_feats])
    grad_first = jnp.einsum(
        "knf,nh->kfh",
        layer_inputs,
        lax.all_gather(grad_pre_low, "feat", axis=1, tiled=True),
        preferred_element_type=jnp.float32,
    )
    summed = lax.psum(
        (grad_first[0], grad_first[1], grad_second_self, grad_second_neigh), ("graph", "dp")
    )
    return (logits[None], summed[0], summed[1], summed[2], summed[3])


def solution(mesh):
    placed = (
        P("dp", "graph", "feat"),
        P("feat", None),
        P("feat", None),
        P("feat", None),
        P("feat", None),
        P("dp", "graph", None, None),
        P("dp", "graph", None, None),
        P("dp", "graph", None),
        P("dp", "graph", None, None, None, None),
        P("dp", "graph", None),
    )
    return jax.shard_map(
        on_device,
        mesh=mesh,
        in_specs=placed,
        out_specs=(
            P("dp", "graph", None),
            P("feat", None),
            P("feat", None),
            P("feat", None),
            P("feat", None),
        ),
        check_vma=False,
    )
```

profile of v0, /device:TPU:1, one launch (start us, length us, event | category | flops | bytes accessed | tf_op | source)
XLA Modules:
  0.0 562.7 jit_solution(8647392232730870567)
XLA Ops:
  7.2 1.4 copy.69
  8.6 10.0 %all-to-all-start = ((s32[16,1,3]{2,1,0:T(1,128)}), s32[16,1,3]{2,1,0:T(1,128)S(1)}, u32[]{:S(2)}, u32[]{:S(2)}) async-start(s32[16,1,3]{2,1,0:T(1,128)} %copy.69), calls=%async_computation | async-start | bytes 16384 | tf_op jit(solution)/shard_map/all_to_all | solution.py:43
  18.6 1.3 copy.81
  20.1 5.4 all-to-all-done
  25.8 2.4 gather_fusion
  28.2 5.0 all-to-all-start.1
  33.9 3.0 fusion.3
  37.1 4.6 fusion.16
  41.7 45.9 %all-to-all-done.1 = bf16[16,3,128,192]{2,3,1,0:T(8,128)(2,1)} async-done(((bf16[16,3,128,192]{2,3,1,0:T(8,128)(2,1)}), bf16[16,3,128,192]{2,3,1,0:T(8,128)(2,1)}, u32[]{:S(2)}, u32[]{:S(2)}) %all-to-all-start.1) | async-done | bytes 2359328 | tf_op jit(solution)/shard_map/all_to_all | solution.py:53
  87.6 6.2 %fusion.40 = f32[16,3,128,192]{3,2,1,0:T(8,128)} fusion(bf16[16,3,128,128]{3,2,1,0:T(8,128)(2,1)S(1)} %get-tuple-element.40, bf16[16,3,128,192]{2,3,1,0:T(8,128)(2,1)} %all-to-all-done.1), kind=kOutput, calls=%fused_computation.65 | convolution fusion | flops 301989888 | bytes 8650752 | tf_op jit(solution)/shard_map/osij,osjw->osiw/dot_general | solution.py:54
  93.8 7.1 %reshape.203 = f32[48,24576]{1,0:T(8,128)} reshape(f32[16,3,128,192]{3,2,1,0:T(8,128)} %fusion.40) | data formatting | bytes 9437184 | tf_op jit(solution)/shard_map/reshape | solution.py:55
  100.9 5.1 fusion.31
  106.0 3.8 reshape.204
  109.8 8.6 %convolution_add_fusion = f32[2048,1024]{1,0:T(8,128)} fusion(f32[2048,1024]{1,0:T(8,128)} %fusion.16, bf16[192,1024]{1,0:T(8,128)(2,1)S(1)} %copy-done.8, f32[2048,192]{1,0:T(8,128)} %reshape.204, f32[2048]{0:T(1024)S(1)} %bitcast.101), kind=kOutput, calls=%fused_computation.3 | convolution fusion | flops 808189952 | bytes 18751488 | tf_op jit(solution)/shard_map/dot_general | solution.py:59
  120.0 2.6 gather_fusion.2
  122.5 4.6 convolution_convert_fusion
  127.1 5.3 all-to-all-start.3
  133.0 0.7 reduce.3
  133.7 69.8 %all-to-all-done.3 = bf16[16,3,128,256]{3,2,1,0:T(8,128)(2,1)} async-done(((bf16[16,3,128,256]{3,2,1,0:T(8,128)(2,1)}), bf16[16,3,128,256]{3,2,1,0:T(8,128)(2,1)}, u32[]{:S(2)}, u32[]{:S(2)}) %all-to-all-start.3) | async-done | bytes 3145760 | tf_op jit(solution)/shard_map/all_to_all | solution.py:80
  203.5 5.6 copy.83
  209.1 2.1 multiply_convert_fusion.2
  211.2 2.6 gather_fusion.1
  213.9 5.4 all-to-all-start.2
  219.3 3.7 fusion.33
  223.1 2.8 reshape.211
  225.8 4.2 fusion.6
  230.5 2.6 copy.84
  233.0 3.7 reshape.208
  236.7 2.7 copy.74
  239.5 2.4 multiply_convert_fusion.4
  241.9 1.6 fusion.41
  243.5 46.9 %all-to-all-done.2 = bf16[16,3,128,256]{3,2,1,0:T(8,128)(2,1)} async-done(((bf16[16,3,128,256]{3,2,1,0:T(8,128)(2,1)}), bf16[16,3,128,256]{3,2,1,0:T(8,128)(2,1)}, u32[]{:S(2)}, u32[]{:S(2)}) %all-to-all-start.2) | async-done | bytes 3145760 | tf_op jit(solution)/shard_map/all_to_all | solution.py:53
  290.4 2.9 fusion.42
  293.3 3.6 copy.82
  296.9 4.0 multiply_convert_fusion
  300.9 2.8 reshape.207
  303.7 3.2 fusion.8
  307.2 1.0 fusion.20
  308.2 1.7 convert_element_type.50
  309.9 1.0 fusion.18
  310.9 4.0 fusion
  314.9 1.2 slice_bitcast_fusion
  316.2 41.8 %all-reduce.4.cloned.1.call-done = f32[1,2048,153]{1,2,0:T(8,128)} async-done(((f32[1,2048,153]{1,2,0:T(8,128)}), f32[1,2048,153]{1,2,0:T(8,128)}) %all-reduce.4.cloned.1.call-update) | async-done | bytes 1253392 | tf_op jit(solution)/shard_map/psum | solution.py:68
  357.9 3.6 copy.77
  361.6 190.2 %all-reduce.6.cloned.1.call-done = (f32[192,1024]{1,0:T(8,128)}, f32[192,1024]{1,0:T(8,128)}, f32[256,153]{0,1:T(8,128)}, f32[256,153]{0,1:T(8,128)}) async-done(((f32[192,1024]{1,0:T(8,128)}, f32[192,1024]{1,0:T(8,128)}, f32[256,153]{0,1:T(8,128)}, f32[256,153]{0,1:T(8,128)}), (f32[192,1024]{1,0:T(8,128)}, f32[192,1024]{1,0:T(8,128)}, f32[256,153]{0,1:T(8,128)}, ...) | async-done | bytes 1886224 | tf_op jit(solution)/shard_map/psum | solution.py:98
  551.8 2.2 copy.94
  554.0 0.9 copy.95
  555.5 0.7 copy.97
  (66 shorter events, 4.8 us)
Async XLA Ops:
  7.2 111.5 %copy-start = (bf16[1,2048,153]{1,2,0:T(8,128)(2,1)S(1)}, bf16[1,2048,153]{1,2,0:T(8,128)(2,1)}, u32[]{:S(2)}) copy-start(bf16[1,2048,153]{1,2,0:T(8,128)(2,1)} %param.19) | copy-start | bytes 1880068
  8.6 16.9 %all-to-all-start = ((s32[16,1,3]{2,1,0:T(1,128)}), s32[16,1,3]{2,1,0:T(1,128)S(1)}, u32[]{:S(2)}, u32[]{:S(2)}) async-start(s32[16,1,3]{2,1,0:T(1,128)} %copy.69), calls=%async_computation | async-start | bytes 16384 | tf_op jit(solution)/shard_map/all_to_all | solution.py:43
  28.2 5.0 copy-start.13
  28.2 5.1 copy-start.14
  28.2 59.4 %all-to-all-start.1 = ((bf16[16,3,128,192]{2,3,1,0:T(8,128)(2,1)}), bf16[16,3,128,192]{2,3,1,0:T(8,128)(2,1)}, u32[]{:S(2)}, u32[]{:S(2)}) async-start(bf16[16,3,128,192]{2,3,1,0:T(8,128)(2,1)} %bitcast.92), calls=%async_computation.1 | async-start | bytes 4718592 | tf_op jit(solution)/shard_map/all_to_all | solution.py:53
  33.2 175.9 %reduce-scatter.2.cloned.1.call-start = ((), (), s32[]{:S(2)}) async-start(), calls=%async_computation.5 | async-start | bytes 10485760 | tf_op jit(solution)/shard_map/reduce_scatter | solution.py:62
  33.9 3.2 copy-start.3
  33.9 3.2 copy-start.7
  106.0 3.8 copy-start.8
  118.4 0.9 copy-start.12
  127.1 76.4 %all-to-all-start.3 = ((bf16[16,3,128,256]{3,2,1,0:T(8,128)(2,1)}), bf16[16,3,128,256]{3,2,1,0:T(8,128)(2,1)}, u32[]{:S(2)}, u32[]{:S(2)}) async-start(bf16[16,3,128,256]{3,2,1,0:T(8,128)(2,1)} %convolution_convert_fusion), calls=%async_computation.4 | async-start | bytes 6291456 | tf_op jit(solution)/shard_map/all_to_all | solution.py:80
  213.9 76.5 %all-to-all-start.2 = ((bf16[16,3,128,256]{3,2,1,0:T(8,128)(2,1)}), bf16[16,3,128,256]{3,2,1,0:T(8,128)(2,1)}, u32[]{:S(2)}, u32[]{:S(2)}) async-start(bf16[16,3,128,256]{3,2,1,0:T(8,128)(2,1)} %bitcast.93), calls=%async_computation.3 | async-start | bytes 6291456 | tf_op jit(solution)/shard_map/all_to_all | solution.py:53
  219.3 91.6 %all-gather.2.cloned.1.call-start = ((), (), s32[]{:S(2)}) async-start(), calls=%async_computation.7 | async-start | bytes 5242880 | tf_op jit(solution)/shard_map/all_gather | solution.py:95
  223.1 2.8 copy-start.11
  230.1 127.8 %all-reduce.4.cloned.1.call-start = ((), (), s32[]{:S(2)}) async-start(), calls=%async_computation.6 | async-start | bytes 2621440 | tf_op jit(solution)/shard_map/psum | solution.py:68
  293.2 3.6 copy-start.1
  300.9 2.8 copy-start.2
  306.9 244.8 %all-reduce.6.cloned.1.call-start = ((), (), s32[]{:S(2)}) async-start(), calls=%async_computation.8 | async-start | bytes 3801088 | tf_op jit(solution)/shard_map/psum | solution.py:98
  308.2 2.7 copy-start.4
  308.2 2.7 copy-start.6
  551.8 2.2 copy-start.5
  551.8 3.1 copy-start.10
  551.8 3.7 copy-start.9
Sparse Core Ops, SparseCore 0:
  118.6 82.1 reduce-scatter.1
  230.2 54.6 all-gather.1
  307.1 50.8 all-reduce.3
  362.2 189.5 all-reduce.5
where the time goes:
time: 565 us; the launch traced here: 563 us
  waiting for transfers between devices  400 us (71%)
  local copies, waits for them, and re-layouts  58.7 us (10%)
  matrix products  55.5 us (10%)
  starting transfers between devices  26.1 us (5%)
  between operations  14 us (2%)
  other arithmetic  8.34 us (1%)
    psum x1, waiting for transfers between devices, on_device(): lax.psum((grad_first[0], grad_first[1], grad_second_self, grad_second_nei...  190 us
    all_to_all x2, waiting for transfers between devices, gather_rows(): lax.all_to_all(picked, 'graph', split_axis=0, concat_axis=0, tiled=True)  92.8 us
    all_to_all x1, waiting for transfers between devices, on_device(): lax.all_to_all(terms, 'graph', split_axis=0, concat_axis=0, tiled=True)  69.8 us
    psum x1, waiting for transfers between devices, on_device(): logits = lax.psum(partial_logits, 'feat')  41.8 us
    unnamed x41, local copies, waits for them, and re-layouts  21.8 us
    reshape x4, local copies, waits for them, and re-layouts, gather_rows(): return summed.reshape(node_count, width)  13.1 us
  transfers between devices with their start and end apart: 8, of which 6 were waited for; matrix products, arithmetic and copies ran while one was open for 14% of the time, Pallas kernels for 0%

commit v1 on v0

v1 whole, which is shorter than its diff:
```python
import functools

import jax
import jax.numpy as jnp
from jax import lax
from jax.experimental import pallas as pl
from jax.experimental.pallas import tpu as pltpu
from jax.sharding import PartitionSpec as P

MESH = pl.DeviceIdType.MESH
TILE = 128
CPAD = 192
BF16, F32, I32 = jnp.bfloat16, jnp.float32, jnp.int32
NT = (((1,), (1,)), ((), ()))


def dot(a, b):
    return jnp.dot(a, b, preferred_element_type=F32)


def dot_nt(a, b):
    return lax.dot_general(a, b, NT, preferred_element_type=F32)


def loop(lo, hi, body):
    def step(i, carry):
        body(i)
        return carry

    lax.fori_loop(lo, hi, step, 0)


def spread_order(k, n):
    return n // 2 + ((k + 0) // 2) * (1 - 2 * (k % 2))


def lanes(start, size):
    return pl.ds(pl.multiple_of(start, TILE), size)


class RingGather:
    def __init__(self, buf, rows, cols, ssem, rsem, x, nx):
        self.buf, self.rows, self.cols, self.ssem, self.rsem, self.x, self.nx = buf, rows, cols, ssem, rsem, x, nx

    def copy(self, owner, first, count, which, to):
        part = self.buf.at[pl.ds(pl.multiple_of(owner * self.rows, 16), self.rows), pl.ds(first, count)]
        return pltpu.make_async_remote_copy(
            src_ref=part,
            dst_ref=part,
            send_sem=self.ssem.at[which],
            recv_sem=self.rsem.at[which],
            device_id={"feat": to},
            device_id_type=MESH,
        )

    def parts(self):
        x, nx, c = self.x, self.nx, self.cols
        right, left = lax.rem(x + 1, nx), lax.rem(x + nx - 1, nx)
        return (
            self.copy(x, 0, c, 0, right),
            self.copy(x, 0, c, 1, left),
            self.copy(left, 0, c // 2, 2, right),
            self.copy(right, c // 2, c // 2, 3, left),
        )

    def start(self):
        a, b, _, _ = self.parts()
        a.start()
        b.start()

    def middle(self):
        a, b, c, d = self.parts()
        a.wait_recv()
        c.start()
        b.wait_recv()
        d.start()

    def finish(self):
        a, b, c, d = self.parts()
        c.wait_recv()
        d.wait_recv()
        for p in (a, b, c, d):
            p.wait_send()


def exchange_kernel(
    n_graph,
    n_feat,
    rows_s,
    count_s,
    cols_v,
    feat_v,
    dl_v,
    bits_v,
    w1s_v,
    w1n_v,
    feat_o,
    ax_o,
    q_o,
    inv_o,
    req_o,
    w1s_o,
    w1n_o,
    featb,
    send,
    arr,
    adj,
    live,
    acc,
    dinv,
    qsend,
    qarr,
    req_s,
    sem_local,
    sem_req_s,
    sem_req_r,
    sem_f_s,
    sem_f_r,
    sem_q_s,
    sem_q_r,
    sem_w_s,
    sem_w_r,
    sem_g_s,
    sem_g_r,
):
    g = lax.axis_index("graph")
    x = lax.axis_index("feat")
    width, nodes = featb.shape[1], feat_o.shape[1]
    n_rows = adj.shape[0]
    row_blocks = n_rows // TILE
    blocks = nodes // TILE
    tpo = 3
    pair = tpo * TILE

    barrier = pltpu.get_barrier_semaphore()

    def greet(d):
        pl.semaphore_signal(barrier, inc=1, device_id={"graph": lax.rem(g + d, n_graph)}, device_id_type=MESH)

    loop(1, n_graph, greet)
    for d in range(1, n_feat):
        pl.semaphore_signal(barrier, inc=1, device_id={"feat": lax.rem(x + d, n_feat)}, device_id_type=MESH)

    iota_r = lax.broadcasted_iota(I32, (width, width), 0)
    iota_c = lax.broadcasted_iota(I32, (width, width), 1)
    eye = (iota_r == iota_c).astype(F32).astype(BF16)
    own_rows = pl.ds(pl.multiple_of(x * width, 16), width)

    def turn(b):
        t = dot_nt(eye, feat_v[pl.ds(pl.multiple_of(b * TILE, TILE), TILE), :]).astype(BF16)
        featb[b] = t
        feat_o[own_rows, lanes(b * TILE, TILE)] = t

    loop(0, blocks, turn)
    req_o[g] = cols_v[g]

    pl.semaphore_wait(barrier, n_graph - 1 + n_feat - 1)

    def request(d):
        to = lax.rem(g + d, n_graph)
        return pltpu.make_async_remote_copy(
            src_ref=cols_v.at[to],
            dst_ref=req_o.at[g],
            send_sem=sem_req_s.at[d],
            recv_sem=sem_req_r.at[d],
            device_id={"graph": to},
            device_id_type=MESH,
        )

    loop(1, n_graph, lambda d: request(d).start())

    gather_feat = RingGather(feat_o, width, nodes, sem_g_s.at[0], sem_g_r.at[0], x, n_feat)
    gather_ax = RingGather(ax_o, width, n_rows, sem_g_s.at[1], sem_g_r.at[1], x, n_feat)
    gather_q = RingGather(q_o, CPAD // n_feat, nodes, sem_g_s.at[2], sem_g_r.at[2], x, n_feat)
    gather_feat.start()

    hidden = w1s_o.shape[1]

    def weights(d, k):
        to = lax.rem(x + d, n_feat)
        src, dst = ((w1s_v, w1s_o), (w1n_v, w1n_o))[k]
        return pltpu.make_async_remote_copy(
            src_ref=src.at[:, lanes(to * hidden, hidden)],
            dst_ref=dst.at[own_rows, :],
            send_sem=sem_w_s.at[k, d],
            recv_sem=sem_w_r.at[k, d],
            device_id={"feat": to},
            device_id_type=MESH,
        )

    deg_ones = jnp.ones((8, TILE), BF16)
    acc_deg = inv_o

    acc_deg[...] = jnp.zeros(acc_deg.shape, F32)

    def prepare(o):
        for s in range(tpo):
            t = o * tpo + s
            on = (s < count_s[o]).astype(I32)
            tile = (bits_v[t] * on).astype(F32)
            live[t] = tile.astype(BF16)

    loop(0, n_graph, prepare)

    def take(d):
        request(d).wait_recv()

    loop(1, n_graph, take)
    fetch = pltpu.make_async_copy(req_o, req_s, sem_local)
    fetch.start()
    fetch.wait()

    def feats(d):
        to = lax.rem(g + d, n_graph)
        return pltpu.make_async_remote_copy(
            src_ref=send.at[to],
            dst_ref=arr.at[g],
            send_sem=sem_f_s.at[d],
            recv_sem=sem_f_r.at[d],
            device_id={"graph": to},
            device_id_type=MESH,
        )

    def post(k):
        d = spread_order(k, n_graph)
        to = lax.rem(g + d, n_graph)
        for s in range(tpo):
            send[to, :, s * TILE : (s + 1) * TILE] = featb[req_s[to, 0, s]]
        feats(d).start()

    loop(1, n_graph, post)
    for s in range(tpo):
        arr[g, :, s * TILE : (s + 1) * TILE] = featb[req_s[g, 0, s]]

    for k in range(2):
        for d in range(1, n_feat):
            weights(d, k).start()
        src, dst = ((w1s_v, w1s_o), (w1n_v, w1n_o))[k]
        dst[own_rows, :] = src[:, lanes(x * hidden, hidden)]

    def build(o):
        for s in range(tpo):
            t = o * tpo + s
            tile = live[t].astype(F32)
            row = rows_s[o, s]
            for r in range(row_blocks):
                here = (row == r).astype(F32)
                adj[r * TILE : (r + 1) * TILE, lanes(t * TILE, TILE)] = (tile * here).astype(BF16)

    loop(0, n_graph, build)

    def degree(o):
        acc_deg[:, :n_rows] += dot_nt(jnp.ones((8, pair), BF16), adj[:, lanes(o * pair, pair)])

    loop(0, n_graph, degree)
    inv_o[...] = 1.0 / jnp.maximum(acc_deg[...], 1.0)

    share = CPAD // n_feat
    own_classes = pl.ds(pl.multiple_of(x * share, 16), share)
    for r in range(row_blocks):
        here = slice(r * TILE, (r + 1) * TILE)
        dinv[r] = (dl_v[own_classes, here].astype(F32) * inv_o[0:1, here]).astype(BF16)

    def q_terms(d):
        to = lax.rem(g + d, n_graph)
        return pltpu.make_async_remote_copy(
            src_ref=qsend.at[to],
            dst_ref=qarr.at[g, pl.ds(0, tpo)],
            send_sem=sem_q_s.at[d],
            recv_sem=sem_q_r.at[d],
            device_id={"graph": to},
            device_id_type=MESH,
        )

    def terms(k):
        d = spread_order(k, n_graph)
        to = lax.rem(g + d, n_graph)
        for s in range(tpo):
            qsend[to, s] = dot(dinv[rows_s[to, s]], live[to * tpo + s]).astype(BF16)
        q_terms(d).start()

    loop(1, n_graph, terms)
    for s in range(tpo):
        qarr[g, s] = dot(dinv[rows_s[g, s]], live[g * tpo + s]).astype(BF16)

    def blank(o):
        qarr[o, tpo] = jnp.zeros((share, TILE), BF16)

    loop(0, n_graph, blank)

    gather_feat.middle()

    def add(o):
        acc[...] += dot_nt(arr[o], adj[:, lanes(o * pair, pair)])

    acc[...] = jnp.zeros(acc.shape, F32)
    add(g)

    def arrive(k):
        d = spread_order(n_graph - k, n_graph)
        feats(d).wait_recv()
        add(lax.rem(g + n_graph - d, n_graph))

    loop(1, n_graph, arrive)
    ax_o[own_rows, :] = (acc[...] * inv_o[0:1, :n_rows]).astype(BF16)
    gather_ax.start()

    loop(1, n_graph, lambda d: q_terms(d).wait_recv())

    def column(c):
        def source(o, total):
            which = jnp.where(
                req_s[o, 0, 0] == c, 0, jnp.where(req_s[o, 0, 1] == c, 1, jnp.where(req_s[o, 0, 2] == c, 2, tpo))
            )
            return total + qarr[o, which].astype(F32)

        total = lax.fori_loop(0, n_graph, source, jnp.zeros((share, TILE), F32))
        q_o[own_classes, lanes(c * TILE, TILE)] = total.astype(BF16)

    loop(0, blocks, column)
    gather_q.start()
    gather_ax.middle()
    gather_q.middle()

    def settle(d):
        request(d).wait_send()
        feats(d).wait_send()
        q_terms(d).wait_send()

    loop(1, n_graph, settle)
    for k in range(2):
        for d in range(1, n_feat):
            weights(d, k).wait()
    gather_feat.finish()
    gather_ax.finish()
    gather_q.finish()


def exchange(n_graph, n_feat, rows, counts, cols, feats, dl_t, bits, w1s, w1n):
    nodes, width = feats.shape
    n_slots, tpo = bits.shape[0], rows.shape[1]
    n_rows = nodes // 4 * 3
    share = CPAD // n_feat
    hidden = w1s.shape[1] // n_feat
    vmem = pl.BlockSpec(memory_space=pltpu.VMEM)
    smem = pl.BlockSpec(memory_space=pltpu.SMEM)
    dma = pltpu.SemaphoreType.DMA
    blocks = nodes // TILE
    cols_wide = jnp.zeros((n_graph, 1, TILE), I32).at[:, 0, :tpo].set(cols)
    return pl.pallas_call(
        functools.partial(exchange_kernel, n_graph, n_feat),
        out_shape=(
            jax.ShapeDtypeStruct((n_feat * width, nodes), BF16),
            jax.ShapeDtypeStruct((n_feat * width, n_rows), BF16),
            jax.ShapeDtypeStruct((CPAD, nodes), BF16),
            jax.ShapeDtypeStruct((8, nodes), F32),
            jax.ShapeDtypeStruct((n_graph, 1, TILE), I32),
            jax.ShapeDtypeStruct((n_feat * width, hidden), BF16),
            jax.ShapeDtypeStruct((n_feat * width, hidden), BF16),
        ),
        in_specs=[smem, smem, vmem, vmem, vmem, vmem, vmem, vmem],
        out_specs=(vmem,) * 7,
        scratch_shapes=[
            pltpu.VMEM((blocks, width, TILE), BF16),
            pltpu.VMEM((n_graph, width, tpo * TILE), BF16),
            pltpu.VMEM((n_graph, width, tpo * TILE), BF16),
            pltpu.VMEM((n_rows, n_slots * TILE), BF16),
            pltpu.VMEM((n_slots, TILE, TILE), BF16),
            pltpu.VMEM((width, n_rows), F32),
            pltpu.VMEM((n_rows // TILE, share, TILE), BF16),
            pltpu.VMEM((n_graph, tpo, share, TILE), BF16),
            pltpu.VMEM((n_graph, tpo + 1, share, TILE), BF16),
            pltpu.SMEM((n_graph, 1, TILE), I32),
            dma,
            dma((n_graph,)),
            dma((n_graph,)),
            dma((n_graph,)),
            dma((n_graph,)),
            dma((n_graph,)),
            dma((n_graph,)),
            dma((2, n_feat)),
            dma((2, n_feat)),
            dma((3, 4)),
            dma((3, 4)),
        ],
        compiler_params=pltpu.CompilerParams(
            collective_id=0, has_side_effects=True, vmem_limit_bytes=56 * 1024 * 1024
        ),
    )(rows, counts, cols_wide, feats, dl_t, bits, w1s, w1n)


def on_device(
    n_graph,
    n_feat,
    features,
    w1_self,
    w1_neigh,
    w2_self,
    w2_neigh,
    tile_rows,
    tile_cols,
    tile_count,
    tile_bits,
    d_logits,
):
    feats = features[0]
    rows, cols, counts = tile_rows[0, 0], tile_cols[0, 0], tile_count[0, 0]
    bits = tile_bits[0, 0].reshape(-1, TILE, TILE)
    nodes = feats.shape[0]
    n_slots, tpo = bits.shape[0], rows.shape[1]
    blocks = nodes // TILE
    n_rows = nodes // 4 * 3
    classes = d_logits.shape[2]
    share = CPAD // n_feat
    dl_t = jnp.pad(d_logits[0].T, ((0, CPAD - classes), (0, 0)))

    feat_t, ax_t, q_t, inv, requested, w1s, w1n = exchange(
        n_graph, n_feat, rows, counts, cols, feats, dl_t, bits, w1_self, w1_neigh
    )
    inv = inv[0]

    w2s = jnp.pad(w2_self, ((0, 0), (0, CPAD - classes)))
    w2n = jnp.pad(w2_neigh, ((0, 0), (0, CPAD - classes)))

    pre = jnp.einsum("fh,fn->hn", w1s, feat_t, preferred_element_type=F32)
    pre = pre + jnp.pad(
        jnp.einsum("fh,fn->hn", w1n, ax_t, preferred_element_type=F32), ((0, 0), (0, nodes - n_rows))
    )
    logistic = jax.nn.sigmoid(pre)
    hidden = (pre * logistic).astype(BF16)
    p_self = jnp.einsum("hc,hn->cn", w2s, hidden, preferred_element_type=F32)
    p_neigh = jnp.einsum("hc,hn->cn", w2n, hidden, preferred_element_type=F32)

    p_neigh = lax.psum_scatter(p_neigh.astype(BF16), "feat", scatter_dimension=0, tiled=True)
    blocked = p_neigh.astype(BF16).reshape(share, blocks, TILE).transpose(1, 0, 2)
    picked = blocked[requested[:, 0, :tpo]]
    arrived = lax.all_to_all(picked, "graph", split_axis=0, concat_axis=0, tiled=True)
    is_live = jnp.arange(tpo, dtype=I32)[None, :] < counts[:, None]
    live_bits = jnp.where(is_live[:, :, None, None], tile_bits[0, 0], 0).astype(BF16)
    terms = jnp.einsum("osij,oscj->osci", live_bits, arrived, preferred_element_type=F32)
    onehot = ((rows[None] == jnp.arange(blocks, dtype=I32)[:, None, None]) & is_live[None]).astype(F32)
    summed = jnp.einsum("ros,osci->cri", onehot, terms, precision=lax.Precision.HIGHEST).reshape(share, nodes)
    p_self = lax.psum_scatter(p_self, "feat", scatter_dimension=0, tiled=True)
    logits_t = lax.all_gather(p_self + inv[None] * summed, "feat", axis=0, tiled=True)
    logits = logits_t[:classes].T

    d_hidden = jnp.einsum("hc,cn->hn", w2s, dl_t, preferred_element_type=F32) + jnp.einsum(
        "hc,cn->hn", w2n, q_t, preferred_element_type=F32
    )
    d_pre = (d_hidden * logistic * (1.0 + pre * (1.0 - logistic))).astype(BF16)
    g1s = jnp.einsum("fn,hn->fh", feat_t, d_pre, preferred_element_type=F32)
    g1n = jnp.einsum("fn,hn->fh", ax_t, d_pre[:, :n_rows], preferred_element_type=F32)
    g2s = jnp.einsum("hn,cn->hc", hidden, dl_t, preferred_element_type=F32)
    g2n = jnp.einsum("hn,cn->hc", hidden, q_t, preferred_element_type=F32)
    g1s = lax.all_to_all(g1s, "feat", split_axis=0, concat_axis=1, tiled=True)
    g1n = lax.all_to_all(g1n, "feat", split_axis=0, concat_axis=1, tiled=True)
    g1s, g1n, g2s, g2n = lax.psum((g1s, g1n, g2s, g2n), ("graph", "dp"))
    return logits[None], g1s, g1n, g2s[:, :classes], g2n[:, :classes]


def solution(mesh):
    placed = (
        P("dp", "graph", "feat"),
        P("feat", None),
        P("feat", None),
        P("feat", None),
        P("feat", None),
        P("dp", "graph", None, None),
        P("dp", "graph", None, None),
        P("dp", "graph", None),
        P("dp", "graph", None, None, None, None),
        P("dp", "graph", None),
    )
    return jax.shard_map(
        functools.partial(on_device, mesh.shape["graph"], mesh.shape["feat"]),
        mesh=mesh,
        in_specs=placed,
        out_specs=(
            P("dp", "graph", None),
            P("feat", None),
            P("feat", None),
            P("feat", None),
            P("feat", None),
        ),
        check_vma=False,
    )
```

time: 565 us -> 392 us (0.69)
  waiting for transfers between devices: 400 us -> 202 us
  Pallas kernels: 0 us -> 111 us
  local copies, waits for them, and re-layouts: 58.7 us -> 22.9 us
  matrix products: 55.5 us -> 21 us
  starting transfers between devices: 26.1 us -> 16.8 us
  other arithmetic: 8.34 us -> 1.97 us
    all_to_all x4 -> x3, waiting for transfers between devices: 168 us -> 33 us  [the longest x1 12.6 us: on_device(): lax.all_to_all(picked, 'graph', split_axis=0, concat_axis=0, tiled=True)]
    pallas_call x0 -> x1, Pallas kernels: none -> 111 us  [exchange(): pl.pallas_call(functools.partial(exchange_kernel, n_graph, n_feat), out_s...]
    psum x2 -> x1, waiting for transfers between devices: 232 us -> 169 us  [on_device(): g1s, g1n, g2s, g2n = lax.psum((g1s, g1n, g2s, g2n), ('graph', 'dp'))]
    dot_general x16 -> x12, matrix products: 55.5 us -> 21 us  [the longest x1 4.07 us: on_device(): g1s = jnp.einsum('fn,hn->fh', feat_t, d_pre, preferred_element_type=F32)]
    reshape x6 -> x0, local copies, waits for them, and re-layouts: 22.9 us -> none  [the longest x4 13.1 us: gather_rows(): return summed.reshape(node_count, width)]
    unnamed x41 -> x39, local copies, waits for them, and re-layouts: 21.8 us -> 9.53 us
    all_to_all x4 -> x3, starting transfers between devices: 25.7 us -> 16.5 us  [the longest x1 9.35 us: on_device(): lax.all_to_all(picked, 'graph', split_axis=0, concat_axis=0, tiled=True)]
    gather x3 -> x1, local copies, waits for them, and re-layouts: 7.62 us -> 1.46 us  [on_device(): picked = blocked[requested[:, 0, :tpo]]]
  transfers between devices with their start and end apart: 8 -> 7, of which waited for: 6 -> 4; matrix products, arithmetic and copies ran while one was open for 14% -> 6% of each run, Pallas kernels for 0% -> 0%
where the time goes in v1:
time: 392 us; the launch traced here: 391 us
  waiting for transfers between devices  202 us (52%)
  Pallas kernels  111 us (28%)
  local copies, waits for them, and re-layouts  22.9 us (6%)
  matrix products  21 us (5%)
  starting transfers between devices  16.8 us (4%)
  between operations  15.4 us (4%)
    psum x1, waiting for transfers between devices, on_device(): g1s, g1n, g2s, g2n = lax.psum((g1s, g1n, g2s, g2n), ('graph', 'dp'))  169 us
    pallas_call x1, Pallas kernels, exchange(): pl.pallas_call(functools.partial(exchange_kernel, n_graph, n_feat), out_s...  111 us
    all_to_all x1, waiting for transfers between devices, on_device(): lax.all_to_all(picked, 'graph', split_axis=0, concat_axis=0, tiled=True)  12.6 us
    all_to_all x1, waiting for transfers between devices, on_device(): g1n = lax.all_to_all(g1n, 'feat', split_axis=0, concat_axis=1, tiled=True)  12.3 us
    unnamed x39, local copies, waits for them, and re-layouts  9.53 us
    all_to_all x1, starting transfers between devices, on_device(): lax.all_to_all(picked, 'graph', split_axis=0, concat_axis=0, tiled=True)  9.35 us
    all_to_all x1, waiting for transfers between devices, on_device(): g1s = lax.all_to_all(g1s, 'feat', split_axis=0, concat_axis=1, tiled=True)  8.12 us
  transfers between devices with their start and end apart: 7, of which 4 were waited for; matrix products, arithmetic and copies ran while one was open for 6% of the time, Pallas kernels for 0%

profile of v1, /device:TPU:1, one launch (start us, length us, event | category | flops | bytes accessed | tf_op | source)
XLA Modules:
  0.0 390.7 jit_solution(6808562213240103303)
XLA Ops:
  8.1 0.7 copy.46
  8.8 0.7 copy.26.rows_s
  9.5 2.2 copy.25
  11.7 0.8 copy.24
  12.4 1.0 pad.21.dl_v
  13.4 0.6 scatter.4.cols_v
  14.0 110.7 %shard_map.137 = (bf16[768,2048]{1,0:T(8,128)(2,1)}, bf16[768,1536]{1,0:T(8,128)(2,1)}, bf16[192,2048]{1,0:T(8,128)(2,1)}, f32[8,2048]{1,0:T(8,128)}, s32[16,1,1...) custom-call(s32[16,3]{1,0:T(8,128)} %copy.26.rows_s, s32[16]{0:T(128)} %bitcast.83, ...), custom_call_target="tpu_custom_call" | custom-call | tf_op jit(solution)/shard_map/pallas_call | solution.py:350
  124.7 2.7 fusion.34
  127.5 2.6 multiply_convert_fusion
  130.1 1.3 convolution_convert_fusion
  131.4 1.6 fusion.17
  133.1 0.5 fusion.15
  133.6 0.6 copy-done.7
  134.2 0.7 copy-done.16
  134.9 1.0 fusion.3
  136.0 0.6 copy-done.4
  136.6 1.7 fusion.10
  138.3 3.5 all-to-all-start.2
  141.8 4.1 %fusion.35 = f32[768,256]{1,0:T(8,128)} fusion(bf16[768,2048]{1,0:T(8,128)(2,1)} %get-tuple-element.25, bf16[256,2048]{1,0:T(8,128)(2,1)} %copy-done.15), kind=kOutput, calls=%fused_computation.48 | convolution fusion | flops 805306368 | bytes 4980736 | tf_op jit(solution)/shard_map/fn,hn->fh/dot_general | solution.py:451
  145.9 12.3 %all-to-all-done.2 = f32[4,192,256]{2,1,0:T(8,128)S(1)} async-done(((f32[4,192,256]{2,1,0:T(8,128)}), f32[4,192,256]{2,1,0:T(8,128)S(1)}, u32[]{:S(2)}, u32[]{:S(2)}) %all-to-all-start.2) | async-done | bytes 786464 | tf_op jit(solution)/shard_map/all_to_all | solution.py:456
  158.1 3.6 all-to-all-start.1
  161.8 0.1 copy.28
  161.9 0.1 copy.29
  162.0 0.1 reshape.140
  162.1 1.0 bitcast_bitcast_fusion
  163.1 1.5 gather_fusion
  164.5 8.1 %all-to-all-done.1 = f32[4,192,256]{2,1,0:T(8,128)S(1)} async-done(((f32[4,192,256]{2,1,0:T(8,128)}), f32[4,192,256]{2,1,0:T(8,128)S(1)}, u32[]{:S(2)}, u32[]{:S(2)}) %all-to-all-start.1) | async-done | bytes 786464 | tf_op jit(solution)/shard_map/all_to_all | solution.py:455
  172.6 9.3 %all-to-all-start = ((bf16[16,3,48,128]{3,2,1,0:T(8,128)(2,1)}), bf16[16,3,48,128]{3,2,1,0:T(8,128)(2,1)}, u32[]{:S(2)}, u32[]{:S(2)}) async-start(bf16[16,3,48,128]{3,2,1,0:T(8,128)(2,1)} %bitcast.76), calls=%async_computation.2 | async-start | bytes 1179648 | tf_op jit(solution)/shard_map/all_to_all | solution.py:437
  182.0 0.1 iota_compare_fusion.1
  182.1 0.1 copy.30
  182.2 0.9 slice.41
  183.1 1.2 fusion.29
  184.3 1.2 fusion.36
  185.5 1.0 copy.39
  186.5 0.4 copy-done.3
  186.9 1.0 copy.38
  187.9 0.2 all-gather.2.cloned.1.call-start
  188.2 12.6 %all-to-all-done = bf16[16,3,48,128]{3,2,1,0:T(8,128)(2,1)} async-done(((bf16[16,3,48,128]{3,2,1,0:T(8,128)(2,1)}), bf16[16,3,48,128]{3,2,1,0:T(8,128)(2,1)}, u32[]{:S(2)}, u32[]{:S(2)}) %all-to-all-start) | async-done | bytes 589856 | tf_op jit(solution)/shard_map/all_to_all | solution.py:437
  200.8 2.3 fusion.4
  203.1 0.8 fusion.8
  203.9 1.9 fusion.12
  205.8 168.9 %all-reduce.8.cloned.1.call-done = (f32[192,1024]{1,0:T(8,128)}, f32[192,1024]{1,0:T(8,128)}, f32[256,192]{0,1:T(8,128)}, f32[256,192]{0,1:T(8,128)}) async-done(((f32[192,1024]{1,0:T(8,128)}, f32[192,1024]{1,0:T(8,128)}, f32[256,192]{0,1:T(8,128)}, f32[256,192]{0,1:T(8,128)}), (f32[192,1024]{1,0:T(8,128)}, f32[192,1024]{1,0:T(8,128)}, f32[256,192]{0,1:T(8,128)}, ...) | async-done | bytes 1966096 | tf_op jit(solution)/shard_map/psum | solution.py:457
  374.8 1.6 slice.51
  376.4 1.6 slice.52
  378.0 1.5 slice_bitcast_fusion
  379.5 2.3 copy.33
  381.8 0.9 copy.51
  382.7 0.9 copy.52
  (42 shorter events, 0.3 us)
Async XLA Ops:
  8.0 4.5 %copy-start.1 = (bf16[1,2048,153]{1,2,0:T(8,128)(2,1)S(1)}, bf16[1,2048,153]{1,2,0:T(8,128)(2,1)}, u32[]{:S(2)}) copy-start(bf16[1,2048,153]{1,2,0:T(8,128)(2,1)} %param.21) | copy-start | bytes 1880068
  8.0 154.1 %reduce-scatter.5.cloned.1.call-start = ((), (), s32[]{:S(2)}) async-start(), calls=%async_computation.6 | async-start | bytes 983040 | tf_op jit(solution)/shard_map/reduce_scatter | solution.py:434
  124.7 2.8 copy-start.13
  124.7 2.8 copy-start.14
  127.5 2.6 copy-start.10
  130.1 1.3 copy-start.9
  131.4 72.5 %reduce-scatter.3.cloned.1.call-start = ((), (), s32[]{:S(2)}) async-start(), calls=%async_computation.5 | async-start | bytes 1966080 | tf_op jit(solution)/shard_map/reduce_scatter | solution.py:443
  133.1 1.1 copy-start.7
  133.1 1.8 copy-start.16
  134.9 1.7 copy-start.4
  136.6 1.7 copy-start.15
  138.3 19.9 %all-to-all-start.2 = ((f32[4,192,256]{2,1,0:T(8,128)}), f32[4,192,256]{2,1,0:T(8,128)S(1)}, u32[]{:S(2)}, u32[]{:S(2)}) async-start(f32[4,192,256]{2,1,0:T(8,128)} %bitcast.19), calls=%async_computation.4 | async-start | bytes 1572864 | tf_op jit(solution)/shard_map/all_to_all | solution.py:456
  141.8 20.0 %copy-start.11 = (s32[16,1,128]{2,1,0:T(1,128)S(1)}, s32[16,1,128]{2,1,0:T(1,128)}, u32[]{:S(2)}) copy-start(s32[16,1,128]{2,1,0:T(1,128)} %get-tuple-element.29) | copy-start | bytes 24580
  158.1 23.9 %copy-start.12 = (s32[1,1,16]{2,1,0:T(1,128)S(1)}, s32[1,1,16]{2,1,0:T(1,128)}, u32[]{:S(2)}) copy-start(s32[1,1,16]{2,1,0:T(1,128)} %param.19) | copy-start | bytes 196
  158.1 14.5 %all-to-all-start.1 = ((f32[4,192,256]{2,1,0:T(8,128)}), f32[4,192,256]{2,1,0:T(8,128)S(1)}, u32[]{:S(2)}, u32[]{:S(2)}) async-start(f32[4,192,256]{2,1,0:T(8,128)} %bitcast.78), calls=%async_computation.3 | async-start | bytes 1572864 | tf_op jit(solution)/shard_map/all_to_all | solution.py:455
  172.6 12.9 %copy-start.2 = (f32[4,192,256]{2,1,0:T(8,128)}, f32[4,192,256]{2,1,0:T(8,128)S(1)}, u32[]{:S(2)}) copy-start(f32[4,192,256]{2,1,0:T(8,128)S(1)} %all-to-all-done.1) | copy-start | bytes 2359300
  172.6 28.1 %all-to-all-start = ((bf16[16,3,48,128]{3,2,1,0:T(8,128)(2,1)}), bf16[16,3,48,128]{3,2,1,0:T(8,128)(2,1)}, u32[]{:S(2)}, u32[]{:S(2)}) async-start(bf16[16,3,48,128]{3,2,1,0:T(8,128)(2,1)} %bitcast.76), calls=%async_computation.2 | async-start | bytes 1179648 | tf_op jit(solution)/shard_map/all_to_all | solution.py:437
  182.0 192.8 %all-reduce.8.cloned.1.call-start = ((), (), s32[]{:S(2)}) async-start(), calls=%async_computation.8 | async-start | bytes 3932160 | tf_op jit(solution)/shard_map/psum | solution.py:457
  182.2 2.1 copy-start.8
  185.5 1.4 copy-start.3
  186.5 14.3 %copy-start = (s32[1,1,16,3,128,128]{5,4,3,2,1,0:T(8,128)S(1)}, s32[1,1,16,3,128,128]{5,4,3,2,1,0:T(8,128)}, u32[]{:S(2)}) copy-start(s32[1,1,16,3,128,128]{5,4,3,2,1,0:T(8,128)} %param.20) | copy-start | bytes 9437188
  187.9 190.0 %all-gather.2.cloned.1.call-start = ((), (), s32[]{:S(2)}) async-start(), calls=%async_computation.7 | async-start | bytes 1966080 | tf_op jit(solution)/shard_map/all_gather | solution.py:444
  378.0 3.9 copy-start.6
  379.5 3.2 copy-start.5
Sparse Core Ops, SparseCore 0:
  131.5 23.7 reduce-scatter.4
  157.8 29.5 reduce-scatter.2
  206.0 23.7 all-gather.1
Sparse Core Ops, SparseCore 1:
  188.0 186.7 all-reduce.7

commit v2 on v1

--- a/solution.py
+++ b/solution.py
@@ -81,6 +81,10 @@
         d.wait_recv()
         for p in (a, b, c, d):
             p.wait_send()
+
+
+def identity(size):
+    return (lax.broadcasted_iota(I32, (size, size), 0) == lax.broadcasted_iota(I32, (size, size), 1)).astype(F32).astype(BF16)
 
 
 def exchange_kernel(
@@ -141,9 +145,7 @@
     for d in range(1, n_feat):
         pl.semaphore_signal(barrier, inc=1, device_id={"feat": lax.rem(x + d, n_feat)}, device_id_type=MESH)
 
-    iota_r = lax.broadcasted_iota(I32, (width, width), 0)
-    iota_c = lax.broadcasted_iota(I32, (width, width), 1)
-    eye = (iota_r == iota_c).astype(F32).astype(BF16)
+    eye = identity(width)
     own_rows = pl.ds(pl.multiple_of(x * width, 16), width)
 
     def turn(b):
@@ -389,9 +391,438 @@
     )(rows, counts, cols_wide, feats, dl_t, bits, w1s, w1n)
 
 
+def update_kernel(
+    n_graph,
+    n_feat,
+    n_dp,
+    rows_s,
+    count_s,
+    req_s,
+    feat_v,
+    ax_v,
+    q_v,
+    dl_v,
+    inv_v,
+    w1s_v,
+    w1n_v,
+    w2s_v,
+    w2n_v,
+    bits_v,
+    logits_o,
+    g1s_o,
+    g1n_o,
+    g2s_o,
+    g2n_o,
+    w1st,
+    w1nt,
+    w2st,
+    w2nt,
+    hid,
+    dpre,
+    pn,
+    ps,
+    pnr,
+    psr,
+    pb,
+    psend,
+    parr,
+    adj,
+    live,
+    acc,
+    lt,
+    grad,
+    cs,
+    cr,
+    ys,
+    yr,
+    xs,
+    tz,
+    zr,
+    fin,
+    sem_p_s,
+    sem_p_r,
+    sem_a_s,
+    sem_a_r,
+    sem_l_s,
+    sem_l_r,
+    sem_c_s,
+    sem_c_r,
+    sem_y_s,
+    sem_y_r,
+    sem_x_s,
+    sem_x_r,
+    sem_z_s,
+    sem_z_r,
+    sem_zg_s,
+    sem_zg_r,
+    sem_yg_s,
+    sem_yg_r,
+    sem_cg_s,
+    sem_cg_r,
+):
+    g = lax.axis_index("graph")
+    x = lax.axis_index("feat")
+    y = lax.axis_index("dp")
+    core = lax.rem(g, 2)
+    z = g // 2
+    n_z = n_graph // 2
+    sibling = g + 1 - 2 * core
+    n_rows = adj.shape[0]
+    row_blocks = n_rows // TILE
+    nodes = feat_v.shape[1]
+    blocks = nodes // TILE
+    hidden = hid.shape[0]
+    width = feat_v.shape[0] // n_feat
+    share = CPAD // n_feat
+    strip = width // n_dp
+    tpo = 3
+    pair = tpo * TILE
+    classes = logits_o.shape[1]
+
+    barrier = pltpu.get_barrier_semaphore()
+
+    def greet(d):
+        pl.semaphore_signal(barrier, inc=1, device_id={"graph": lax.rem(g + d, n_graph)}, device_id_type=MESH)
+
+    loop(1, n_graph, greet)
+    for d in range(1, n_feat):
+        pl.semaphore_signal(barrier, inc=1, device_id={"feat": lax.rem(x + d, n_feat)}, device_id_type=MESH)
+    for d in range(1, n_dp):
+        pl.semaphore_signal(barrier, inc=1, device_id={"dp": lax.rem(y + d, n_dp)}, device_id_type=MESH)
+
+    def send(src, dst, ssem, rsem, to):
+        return pltpu.make_async_remote_copy(
+            src_ref=src, dst_ref=dst, send_sem=ssem, recv_sem=rsem, device_id=to, device_id_type=MESH
+        )
+
+    eye = identity(hidden)
+    w1st[...] = dot_nt(eye, w1s_v[...]).astype(BF16)
+    w1nt[...] = dot_nt(eye, w1n_v[...]).astype(BF16)
+    eye_c = identity(CPAD)
+    w2st[...] = dot_nt(eye_c, w2s_v[...]).astype(BF16)
+    w2nt[...] = dot_nt(eye_c, w2n_v[...]).astype(BF16)
+
+    chunk = nodes // 4
+
+    def layer(n, with_neighbours):
+        here = lanes(n * chunk, chunk)
+        pre = dot(w1st[...], feat_v[:, here])
+        if with_neighbours:
+            pre = pre + dot(w1nt[...], ax_v[:, here])
+        sig = 1.0 / (1.0 + jnp.exp(-pre))
+        act = (pre * sig).astype(BF16)
+        hid[:, here] = act
+        pn[:, here] = dot(w2nt[...], act).astype(BF16)
+        ps[:, here] = dot(w2st[...], act).astype(BF16)
+        back = dot(w2s_v[...], dl_v[:, here]) + dot(w2n_v[...], q_v[:, here])
+        dpre[:, here] = (back * sig * (1.0 + pre * (1.0 - sig))).astype(BF16)
+
+    loop(0, 3, lambda n: layer(n, True))
+    layer(3, False)
+
+    pl.semaphore_wait(barrier, n_graph - 1 + n_feat - 1 + n_dp - 1)
+
+    def scatter(d, k):
+        to = lax.rem(x + d, n_feat)
+        src, dst = ((pn, pnr), (ps, psr))[k]
+        return send(
+            src.at[pl.ds(pl.multiple_of(to * share, 16), share), :],
+            dst.at[x],
+            sem_p_s.at[k, d],
+            sem_p_r.at[k, d],
+            {"feat": to},
+        )
+
+    for d in range(1, n_feat):
+        scatter(d, 0).start()
+
+    def gradients(k):
+        src, cols, other = ((feat_v, nodes, dl_v), (ax_v, n_rows, q_v))[k]
+        dp = dpre[:, :cols]
+
+        def first(o):
+            t = dot_nt(src[pl.ds(pl.multiple_of(o * width, 16), width), :], dp)
+            for i in range(n_dp):
+                grad[k, i, pl.ds(pl.multiple_of(o * strip, 16), strip), :] = t[i * strip : (i + 1) * strip]
+
+        loop(0, n_feat, first)
+        t = dot_nt(other[...], hid[...])
+        for i in range(n_dp):
+            grad[k, i, n_feat * strip :, :] = t[i * share : (i + 1) * share]
+
+    gradients(0)
+    gradients(1)
+    cs[...] = grad[1 - core].astype(BF16)
+    core_send = send(cs, cr, sem_c_s, sem_c_r, {"graph": sibling})
+    core_send.start()
+    for d in range(1, n_feat):
+        scatter(d, 1).start()
+
+    def prepare(o):
+        for s in range(tpo):
+            t = o * tpo + s
+            on = (s < count_s[o]).astype(I32)
+            tile = (bits_v[t] * on).astype(F32)
+            row = rows_s[o, s]
+            for r in range(row_blocks):
+                here = (row == r).astype(F32)
+                adj[r * TILE : (r + 1) * TILE, lanes(t * TILE, TILE)] = (tile * here).astype(BF16)
+
+    loop(0, n_graph, prepare)
+
+    for d in range(1, n_feat):
+        scatter(d, 0).wait_recv()
+    own_classes = pl.ds(pl.multiple_of(x * share, 16), share)
+    pnr[x] = pn[own_classes, :]
+    for b in range(blocks):
+        here = slice(b * TILE, (b + 1) * TILE)
+        total = pnr[0, :, here].astype(F32)
+        for o in range(1, n_feat):
+            total = total + pnr[o, :, here].astype(F32)
+        pb[b] = total.astype(BF16)
+
+    def scores(d):
+        to = lax.rem(g + d, n_graph)
+        return send(psend.at[to], parr.at[g], sem_a_s.at[d], sem_a_r.at[d], {"graph": to})
+
+    def post(k):
+        d = spread_order(k, n_graph)
+        to = lax.rem(g + d, n_graph)
+        for s in range(tpo):
+            psend[to, :, s * TILE : (s + 1) * TILE] = pb[req_s[to, 0, s]]
+        scores(d).start()
+
+    loop(1, n_graph, post)
+    for s in range(tpo):
+        parr[g, :, s * TILE : (s + 1) * TILE] = pb[req_s[g, 0, s]]
+
+    core_send.wait_recv()
+    for i in range(n_dp):
+        grad[core, i] = grad[core, i] + cr[i].astype(F32)
+        ys[i] = grad[core, i].astype(BF16)
+
+    def over_y(d):
+        to = lax.rem(y + d, n_dp)
+        return send(ys.at[to], yr.at[y], sem_y_s.at[d], sem_y_r.at[d], {"dp": to})
+
+    for d in range(1, n_dp):
+        over_y(d).start()
+
+    for d in range(1, n_feat):
+        scatter(d, 1).wait_recv()
+
+    for d in range(1, n_dp):
+        over_y(d).wait_recv()
+    total = grad[core, y]
+    for d in range(1, n_dp):
+        total = total + yr[lax.rem(y + d, n_dp)].astype(F32)
+    low = total.astype(BF16)
+    top = n_feat * strip
+    xs[...] = low[:top]
+    tz[top : top + share, :] = low[top:]
+    tz[top + share :, :] = jnp.zeros((tz.shape[0] - top - share, hidden), BF16)
+
+    def over_x(d):
+        to = lax.rem(x + d, n_feat)
+        return send(
+            xs.at[pl.ds(pl.multiple_of(to * strip, 16), strip), :],
+            tz.at[pl.ds(pl.multiple_of(x * strip, 16), strip), :],
+            sem_x_s.at[d],
+            sem_x_r.at[d],
+            {"feat": to},
+        )
+
+    for d in range(1, n_feat):
+        over_x(d).start()
+    own_strip = pl.ds(pl.multiple_of(x * strip, 16), strip)
+    tz[own_strip, :] = xs[own_strip, :]
+    for d in range(1, n_feat):
+        over_x(d).wait_recv()
+
+    piece = tz.shape[0] // n_z
+
+    def rows_of(o):
+        return pl.ds(pl.multiple_of(o * piece, 16), piece)
+
+    def over_z(d):
+        to = lax.rem(z + d, n_z)
+        return send(tz.at[rows_of(to), :], zr.at[z], sem_z_s.at[d], sem_z_r.at[d], {"graph": to * 2 + core})
+
+    loop(1, n_z, lambda d: over_z(d).start())
+
+    acc[...] = dot_nt(parr[g], adj[:, lanes(g * pair, pair)])
+
+    def arrive(k):
+        d = spread_order(n_graph - k, n_graph)
+        scores(d).wait_recv()
+        o = lax.rem(g + n_graph - d, n_graph)
+        acc[...] += dot_nt(parr[o], adj[:, lanes(o * pair, pair)])
+
+    loop(1, n_graph, arrive)
+
+    psr[x] = ps[own_classes, :]
+    for b in range(blocks):
+        here = slice(b * TILE, (b + 1) * TILE)
+        total = psr[0, :, here].astype(F32)
+        for o in range(1, n_feat):
+            total = total + psr[o, :, here].astype(F32)
+        if b < row_blocks:
+            total = total + acc[:, here] * inv_v[0:1, here]
+        lt[own_classes, here] = total.astype(BF16)
+    gather_l = RingGather(lt, share, nodes, sem_l_s, sem_l_r, x, n_feat)
+    gather_l.start()
+
+    loop(1, n_z, lambda d: over_z(d).wait_recv())
+    total = tz[rows_of(z), :].astype(F32)
+    for d in range(1, n_z):
+        total = total + zr[lax.rem(z + d, n_z)].astype(F32)
+    fin[core, y, rows_of(z), :] = total.astype(BF16)
+
+    def spread_z(d):
+        part = fin.at[core, y, rows_of(z), :]
+        return send(part, part, sem_zg_s.at[d], sem_zg_r.at[d], {"graph": lax.rem(z + d, n_z) * 2 + core})
+
+    loop(1, n_z, lambda d: spread_z(d).start())
+    gather_l.middle()
+    loop(1, n_z, lambda d: spread_z(d).wait_recv())
+
+    def spread_y(d):
+        part = fin.at[core, y]
+        return send(part, part, sem_yg_s.at[d], sem_yg_r.at[d], {"dp": lax.rem(y + d, n_dp)})
+
+    def spread_core(d):
+        part = fin.at[core, lax.rem(y + n_dp - d, n_dp)]
+        return send(part, part, sem_cg_s.at[d], sem_cg_r.at[d], {"graph": sibling})
+
+    for d in range(1, n_dp):
+        spread_y(d).start()
+    spread_core(0).start()
+    gather_l.finish()
+    eye_n = identity(TILE)
+
+    def turn(b):
+        t = dot_nt(eye_n, lt[:, lanes(b * TILE, TILE)])
+        logits_o[pl.ds(pl.multiple_of(b * TILE, TILE), TILE), :] = t[:, :classes]
+
+    loop(0, blocks, turn)
+    for d in range(1, n_dp):
+        spread_y(d).wait_recv()
+        spread_core(d).start()
+    for d in range(n_dp):
+        spread_core(d).wait_recv()
+
+    for k, first, second in ((0, g1s_o, g2s_o), (1, g1n_o, g2n_o)):
+        for i in range(n_dp):
+            for o in range(n_feat):
+                first[i * strip : (i + 1) * strip, o * hidden : (o + 1) * hidden] = fin[
+                    k, i, o * strip : (o + 1) * strip, :
+                ].astype(F32)
+        stacked = jnp.concatenate([fin[k, i, top : top + share, :] for i in range(n_dp)], axis=0)
+        second[...] = dot_nt(eye, stacked)[:, :classes]
+
+    core_send.wait_send()
+    for d in range(1, n_feat):
+        scatter(d, 0).wait_send()
+        scatter(d, 1).wait_send()
+        over_x(d).wait_send()
+    for d in range(1, n_dp):
+        over_y(d).wait_send()
+        spread_y(d).wait_send()
+    for d in range(n_dp):
+        spread_core(d).wait_send()
+
+    loop(1, n_graph, lambda d: scores(d).wait_send())
+
+    def settle(d):
+        over_z(d).wait_send()
+        spread_z(d).wait_send()
+
+    loop(1, n_z, settle)
+
+
+def update(n_graph, n_feat, n_dp, rows, counts, requested, feat_t, ax_t, q_t, dl_t, inv, w1s, w1n, w2s, w2n, bits, classes):
+    nodes, n_rows = feat_t.shape[1], ax_t.shape[1]
+    width = feat_t.shape[0] // n_feat
+    hidden = w1s.shape[1]
+    n_slots, tpo = bits.shape[0], rows.shape[1]
+    share = CPAD // n_feat
+    strip = width // n_dp
+    n_z = n_graph // 2
+    held = n_feat * strip + share
+    padded = -(-held // (16 * n_z)) * 16 * n_z
+    vmem = pl.BlockSpec(memory_space=pltpu.VMEM)
+    smem = pl.BlockSpec(memory_space=pltpu.SMEM)
+    dma = pltpu.SemaphoreType.DMA
+    blocks = nodes // TILE
+    return pl.pallas_call(
+        functools.partial(update_kernel, n_graph, n_feat, n_dp),
+        out_shape=(
+            jax.ShapeDtypeStruct((nodes, classes), F32),
+            jax.ShapeDtypeStruct((width, n_feat * hidden), F32),
+            jax.ShapeDtypeStruct((width, n_feat * hidden), F32),
+            jax.ShapeDtypeStruct((hidden, classes), F32),
+            jax.ShapeDtypeStruct((hidden, classes), F32),
+        ),
+        in_specs=[smem] * 3 + [vmem] * 10,
+        out_specs=(vmem,) * 5,
+        scratch_shapes=[
+            pltpu.VMEM((hidden, n_feat * width), BF16),
+            pltpu.VMEM((hidden, n_feat * width), BF16),
+            pltpu.VMEM((CPAD, hidden), BF16),
+            pltpu.VMEM((CPAD, hidden), BF16),
+            pltpu.VMEM((hidden, nodes), BF16),
+            pltpu.VMEM((hidden, nodes), BF16),
+            pltpu.VMEM((CPAD, nodes), BF16),
+            pltpu.VMEM((CPAD, nodes), BF16),
+            pltpu.VMEM((n_feat, share, nodes), BF16),
+            pltpu.VMEM((n_feat, share, nodes), BF16),
+            pltpu.VMEM((blocks, share, TILE), BF16),
+            pltpu.VMEM((n_graph, share, tpo * TILE), BF16),
+            pltpu.VMEM((n_graph, share, tpo * TILE), BF16),
+            pltpu.VMEM((n_rows, n_slots * TILE), BF16),
+            pltpu.VMEM((8, TILE), BF16),
+            pltpu.VMEM((share, n_rows), F32),
+            pltpu.VMEM((CPAD, nodes), BF16),
+            pltpu.VMEM((2, n_dp, held, hidden), F32),
+            pltpu.VMEM((n_dp, held, hidden), BF16),
+            pltpu.VMEM((n_dp, held, hidden), BF16),
+            pltpu.VMEM((n_dp, held, hidden), BF16),
+            pltpu.VMEM((n_dp, held, hidden), BF16),
+            pltpu.VMEM((n_feat * strip, hidden), BF16),
+            pltpu.VMEM((padded, hidden), BF16),
+            pltpu.VMEM((n_z, padded // n_z, hidden), BF16),
+            pltpu.VMEM((2, n_dp, padded, hidden), BF16),
+            dma((2, n_feat)),
+            dma((2, n_feat)),
+            dma((n_graph,)),
+            dma((n_graph,)),
+            dma((4,)),
+            dma((4,)),
+            dma,
+            dma,
+            dma((n_dp,)),
+            dma((n_dp,)),
+            dma((n_feat,)),
+            dma((n_feat,)),
+            dma((n_z,)),
+            dma((n_z,)),
+            dma((n_z,)),
+            dma((n_z,)),
+            dma((n_dp,)),
+            dma((n_dp,)),
+            dma((n_dp,)),
+            dma((n_dp,)),
+        ],
+        compiler_params=pltpu.CompilerParams(
+            collective_id=1, has_side_effects=True, vmem_limit_bytes=58 * 1024 * 1024
+        ),
+    )(rows, counts, requested, feat_t, ax_t, q_t, dl_t, inv, w1s, w1n, w2s, w2n, bits)
+
+
 def on_device(
     n_graph,
     n_feat,
+    n_dp,
     features,
     w1_self,
     w1_neigh,
@@ -406,56 +837,18 @@
     feats = features[0]
     rows, cols, counts = tile_rows[0, 0], tile_cols[0, 0], tile_count[0, 0]
     bits = tile_bits[0, 0].reshape(-1, TILE, TILE)
-    nodes = feats.shape[0]
-    n_slots, tpo = bits.shape[0], rows.shape[1]
-    blocks = nodes // TILE
-    n_rows = nodes // 4 * 3
     classes = d_logits.shape[2]
-    share = CPAD // n_feat
     dl_t = jnp.pad(d_logits[0].T, ((0, CPAD - classes), (0, 0)))
 
     feat_t, ax_t, q_t, inv, requested, w1s, w1n = exchange(
         n_graph, n_feat, rows, counts, cols, feats, dl_t, bits, w1_self, w1_neigh
     )
-    inv = inv[0]
-
     w2s = jnp.pad(w2_self, ((0, 0), (0, CPAD - classes)))
     w2n = jnp.pad(w2_neigh, ((0, 0), (0, CPAD - classes)))
-
-    pre = jnp.einsum("fh,fn->hn", w1s, feat_t, preferred_element_type=F32)
-    pre = pre + jnp.pad(
-        jnp.einsum("fh,fn->hn", w1n, ax_t, preferred_element_type=F32), ((0, 0), (0, nodes - n_rows))
+    logits, g1s, g1n, g2s, g2n = update(
+        n_graph, n_feat, n_dp, rows, counts, requested, feat_t, ax_t, q_t, dl_t, inv, w1s, w1n, w2s, w2n, bits, classes
     )
-    logistic = jax.nn.sigmoid(pre)
-    hidden = (pre * logistic).astype(BF16)
-    p_self = jnp.einsum("hc,hn->cn", w2s, hidden, preferred_element_type=F32)
-    p_neigh = jnp.einsum("hc,hn->cn", w2n, hidden, preferred_element_type=F32)
-
-    p_neigh = lax.psum_scatter(p_neigh.astype(BF16), "feat", scatter_dimension=0, tiled=True)
-    blocked = p_neigh.astype(BF16).reshape(share, blocks, TILE).transpose(1, 0, 2)
-    picked = blocked[requested[:, 0, :tpo]]
-    arrived = lax.all_to_all(picked, "graph", split_axis=0, concat_axis=0, tiled=True)
-    is_live = jnp.arange(tpo, dtype=I32)[None, :] < counts[:, None]
-    live_bits = jnp.where(is_live[:, :, None, None], tile_bits[0, 0], 0).astype(BF16)
-    terms = jnp.einsum("osij,oscj->osci", live_bits, arrived, preferred_element_type=F32)
-    onehot = ((rows[None] == jnp.arange(blocks, dtype=I32)[:, None, None]) & is_live[None]).astype(F32)
-    summed = jnp.einsum("ros,osci->cri", onehot, terms, precision=lax.Precision.HIGHEST).reshape(share, nodes)
-    p_self = lax.psum_scatter(p_self, "feat", scatter_dimension=0, tiled=True)
-    logits_t = lax.all_gather(p_self + inv[None] * summed, "feat", axis=0, tiled=True)
-    logits = logits_t[:classes].T
-
-    d_hidden = jnp.einsum("hc,cn->hn", w2s, dl_t, preferred_element_type=F32) + jnp.einsum(
-        "hc,cn->hn", w2n, q_t, preferred_element_type=F32
-    )
-    d_pre = (d_hidden * logistic * (1.0 + pre * (1.0 - logistic))).astype(BF16)
-    g1s = jnp.einsum("fn,hn->fh", feat_t, d_pre, preferred_element_type=F32)
-    g1n = jnp.einsum("fn,hn->fh", ax_t, d_pre[:, :n_rows], preferred_element_type=F32)
-    g2s = jnp.einsum("hn,cn->hc", hidden, dl_t, preferred_element_type=F32)
-    g2n = jnp.einsum("hn,cn->hc", hidden, q_t, preferred_element_type=F32)
-    g1s = lax.all_to_all(g1s, "feat", split_axis=0, concat_axis=1, tiled=True)
-    g1n = lax.all_to_all(g1n, "feat", split_axis=0, concat_axis=1, tiled=True)
-    g1s, g1n, g2s, g2n = lax.psum((g1s, g1n, g2s, g2n), ("graph", "dp"))
-    return logits[None], g1s, g1n, g2s[:, :classes], g2n[:, :classes]
+    return logits[None], g1s, g1n, g2s, g2n
 
 
 def solution(mesh):
@@ -472,7 +865,7 @@
         P("dp", "graph", None),
     )
     return jax.shard_map(
-        functools.partial(on_device, mesh.shape["graph"], mesh.shape["feat"]),
+        functools.partial(on_device, mesh.shape["graph"], mesh.shape["feat"], mesh.shape["dp"]),
         mesh=mesh,
         in_specs=placed,
         out_specs=(

time: 392 us -> 193 us (0.49)
  waiting for transfers between devices: 202 us -> 0 us
  Pallas kernels: 111 us -> 175 us
  matrix products: 21 us -> 0 us
  starting transfers between devices: 16.8 us -> 0 us
  between operations: 15.4 us -> 0.71 us
  local copies, waits for them, and re-layouts: 22.9 us -> 16.9 us
    psum x1 -> x0, waiting for transfers between devices: 169 us -> none  [on_device(): g1s, g1n, g2s, g2n = lax.psum((g1s, g1n, g2s, g2n), ('graph', 'dp'))]
    pallas_call x0 -> x1, Pallas kernels: none -> 64 us  [update(): pl.pallas_call(functools.partial(update_kernel, n_graph, n_feat, n_dp), o...]
    all_to_all x3 -> x0, waiting for transfers between devices: 33 us -> none  [the longest x1 12.6 us: on_device(): lax.all_to_all(picked, 'graph', split_axis=0, concat_axis=0, tiled=True)]
    dot_general x12 -> x0, matrix products: 21 us -> none  [the longest x1 4.07 us: on_device(): g1s = jnp.einsum('fn,hn->fh', feat_t, d_pre, preferred_element_type=F32)]
    all_to_all x3 -> x0, starting transfers between devices: 16.5 us -> none  [the longest x1 9.35 us: on_device(): lax.all_to_all(picked, 'graph', split_axis=0, concat_axis=0, tiled=True)]
    slice x4 -> x0, local copies, waits for them, and re-layouts: 4.19 us -> none  [the longest x2 3.18 us: on_device(): return (logits[None], g1s, g1n, g2s[:, :classes], g2n[:, :classes])]
    unnamed x39 -> x18, local copies, waits for them, and re-layouts: 9.53 us -> 10.7 us
  transfers between devices with their start and end apart: 7 -> 0, of which waited for: 4 -> 0; matrix products, arithmetic and copies ran while one was open for 6% -> 0% of each run, Pallas kernels for 0% -> 0%
where the time goes in v2:
time: 193 us; the launch traced here: 192 us
  Pallas kernels  175 us (91%)
  local copies, waits for them, and re-layouts  16.9 us (9%)
    pallas_call x1, Pallas kernels, exchange(): pl.pallas_call(functools.partial(exchange_kernel, n_graph, n_feat), out_s...  111 us
    pallas_call x1, Pallas kernels, update(): pl.pallas_call(functools.partial(update_kernel, n_graph, n_feat, n_dp), o...  64 us
    unnamed x18, local copies, waits for them, and re-layouts  10.7 us

profile of v2, /device:TPU:1, one launch (start us, length us, event | category | flops | bytes accessed | tf_op | source)
XLA Modules:
  0.0 192.3 jit_solution(16517017574072950807)
XLA Ops:
  0.6 0.0 copy-start
  0.6 1.4 copy.24
  2.1 0.8 copy.15
  2.8 0.6 scatter.4.cols_v
  3.4 1.0 copy.18
  4.4 0.7 pad.17.w2s_v
  5.1 1.0 copy.19
  6.1 0.7 pad.18.w2n_v
  6.8 2.0 %pad.16.dl_v = bf16[192,2048]{1,0:T(8,128)(2,1)} pad(bf16[153,2048]{1,0:T(8,128)(2,1)} %bitcast.13, bf16[]{:T(256)} %constant.32.clone.1), padding=0_39x0_0 | pad | bytes 1413122 | tf_op jit(solution)/shard_map/jit(_pad)/pad | solution.py:841
  8.8 0.0 copy-done
  8.8 1.3 copy.16
  10.1 110.7 %shard_map.137 = (bf16[768,2048]{1,0:T(8,128)(2,1)}, bf16[768,1536]{1,0:T(8,128)(2,1)}, bf16[192,2048]{1,0:T(8,128)(2,1)}, f32[8,2048]{1,0:T(8,128)}, s32[16,1,1...) custom-call(s32[16,3]{1,0:T(8,128)} %bitcast.14, s32[16]{0:T(128)} %bitcast.16, ...), custom_call_target="tpu_custom_call" | custom-call | tf_op jit(solution)/shard_map/pallas_call | solution.py:352
  120.8 64.0 %shard_map.138 = (f32[2048,153]{1,0:T(8,128)}, f32[192,1024]{1,0:T(8,128)}, f32[192,1024]{1,0:T(8,128)}, f32[256,153]{1,0:T(8,128)}, f32[256,153]{1,0:T(8,128)}) custom-call(s32[16,3]{1,0:T(8,128)} %bitcast.15, s32[16]{0:T(128)} %bitcast.17, s32[16,1,128]{2,1,0:T(1,128)} %get-tuple-element.29.req_s, bf16[768,2048]{1,0:T(8,128)(2,1)} %get-tuple-element.30.feat_v, ...), custom_call_target="tpu_custom_call" | custom-call | tf_op jit(solution)/shard_map/pallas_call | solution.py:757
  184.8 0.0 copy-start.4
  184.8 0.0 copy-start.3
  184.8 0.0 copy-start.2
  184.8 0.0 copy-start.1
  184.8 4.1 %copy.21 = f32[1,2048,153]{1,0,2:T(1,128)} copy(f32[1,2048,153]{2,1,0:T(8,128)} %bitcast.12) | data formatting | bytes 2506752
  188.9 0.0 copy-done.4
  188.9 0.8 copy.22
  189.7 0.0 copy-done.3
  189.7 0.8 copy.23
  190.5 0.0 copy-done.2
  190.5 0.9 copy.27
  191.4 0.0 copy-done.1
  191.4 0.9 copy.28
Async XLA Ops:
  0.6 8.2 %copy-start = (bf16[1,2048,192]{1,2,0:T(8,128)(2,1)S(1)}, bf16[1,2048,192]{1,2,0:T(8,128)(2,1)}, u32[]{:S(2)}) copy-start(bf16[1,2048,192]{1,2,0:T(8,128)(2,1)} %param.12) | copy-start | bytes 2359300
  184.8 4.1 %copy-start.4 = (f32[256,153]{1,0:T(8,128)S(1)}, f32[256,153]{1,0:T(8,128)}, u32[]{:S(2)}) copy-start(f32[256,153]{1,0:T(8,128)} %get-tuple-element.44) | copy-start | bytes 470020
  184.8 4.9 %copy-start.3 = (f32[256,153]{1,0:T(8,128)S(1)}, f32[256,153]{1,0:T(8,128)}, u32[]{:S(2)}) copy-start(f32[256,153]{1,0:T(8,128)} %get-tuple-element.45) | copy-start | bytes 470020
  184.8 5.7 %copy-start.2 = (f32[192,1024]{1,0:T(8,128)S(1)}, f32[192,1024]{1,0:T(8,128)}, u32[]{:S(2)}) copy-start(f32[192,1024]{1,0:T(8,128)} %get-tuple-element.52) | copy-start | bytes 2359300
  184.8 6.5 %copy-start.1 = (f32[192,1024]{1,0:T(8,128)S(1)}, f32[192,1024]{1,0:T(8,128)}, u32[]{:S(2)}) copy-start(f32[192,1024]{1,0:T(8,128)} %get-tuple-element.53) | copy-start | bytes 2359300

commit v3 on v0

v3 whole, which is shorter than its diff:
```python
import functools

import jax
import jax.numpy as jnp
from jax import lax
from jax.experimental import pallas as pl
from jax.experimental.pallas import tpu as pltpu
from jax.sharding import PartitionSpec as P

MESH = pl.DeviceIdType.MESH
TILE = 128
TPO = 3
CPAD = 192
PARTS = 2
BF16, F32, I32 = jnp.bfloat16, jnp.float32, jnp.int32
NT = (((1,), (1,)), ((), ()))


def dot(a, b):
    return jnp.dot(a, b, preferred_element_type=F32)


def dot_nt(a, b):
    return lax.dot_general(a, b, NT, preferred_element_type=F32)


def loop(lo, hi, body):
    def step(i, carry):
        body(i)
        return carry

    lax.fori_loop(lo, hi, step, 0)


def spread_order(k, n):
    return n // 2 + (k // 2) * (1 - 2 * (k % 2))


def lanes(start, size):
    return pl.ds(pl.multiple_of(start, TILE), size)


def rows_at(start, size):
    return pl.ds(pl.multiple_of(start, 16), size)


def identity(rows, cols):
    same = lax.broadcasted_iota(I32, (rows, cols), 0) == lax.broadcasted_iota(I32, (rows, cols), 1)
    return same.astype(F32).astype(BF16)


def remote(src, dst, ssem, rsem, to):
    return pltpu.make_async_remote_copy(
        src_ref=src, dst_ref=dst, send_sem=ssem, recv_sem=rsem, device_id=to, device_id_type=MESH
    )


class RingGather:
    def __init__(self, buf, base, stride, rows, ssem, rsem, x, nx, axis="feat"):
        self.buf, self.base, self.stride, self.rows, self.axis = buf, base, stride, rows, axis
        self.ssem, self.rsem, self.x, self.nx = ssem, rsem, x, nx
        self.cols = buf.shape[1]

    def copy(self, owner, first, count, which, to):
        part = self.buf.at[rows_at(self.base + owner * self.stride, self.rows), pl.ds(first, count)]
        return remote(part, part, self.ssem.at[which], self.rsem.at[which], {self.axis: to})

    def parts(self):
        x, nx, c = self.x, self.nx, self.cols
        right, left = lax.rem(x + 1, nx), lax.rem(x + nx - 1, nx)
        return (
            self.copy(x, 0, c, 0, right),
            self.copy(x, 0, c, 1, left),
            self.copy(left, 0, c // 2, 2, right),
            self.copy(right, c // 2, c // 2, 3, left),
        )

    def start(self):
        a, b, _, _ = self.parts()
        a.start()
        b.start()

    def middle(self):
        a, b, c, d = self.parts()
        a.wait_recv()
        c.start()
        b.wait_recv()
        d.start()

    def arrive(self):
        _, _, c, d = self.parts()
        c.wait_recv()
        d.wait_recv()

    def settle(self):
        for p in self.parts():
            p.wait_send()


def step_kernel(
    n_graph,
    n_feat,
    n_dp,
    rows_s,
    count_s,
    cols_v,
    feat_v,
    dl_v,
    w2s_v,
    w2n_v,
    bits_h,
    w1s_h,
    w1n_h,
    lt,
    first_o,
    second_o,
    fin,
    bits,
    featb,
    featf,
    axf,
    send,
    arr,
    adj,
    acc,
    deg,
    dinv,
    qsend,
    qarr,
    cols_w,
    req_v,
    req_s,
    w1f,
    w1t,
    w2t,
    w2c,
    dq,
    pre,
    hid,
    dpre,
    pp,
    pr,
    pb,
    psend,
    parr,
    pacc,
    grad,
    cr,
    ys,
    yr,
    xs,
    tz,
    zr,
    sem_local,
    sem_req_s,
    sem_req_r,
    sem_f_s,
    sem_f_r,
    sem_q_s,
    sem_q_r,
    sem_w_s,
    sem_w_r,
    sem_g_s,
    sem_g_r,
    sem_p_s,
    sem_p_r,
    sem_a_s,
    sem_a_r,
    sem_c_s,
    sem_c_r,
    sem_y_s,
    sem_y_r,
    sem_x_s,
    sem_x_r,
    sem_z_s,
    sem_z_r,
    sem_zg_s,
    sem_zg_r,
    sem_yg_s,
    sem_yg_r,
    sem_cg_s,
    sem_cg_r,
):
    g = lax.axis_index("graph")
    x = lax.axis_index("feat")
    y = lax.axis_index("dp")
    core = lax.rem(g, 2)
    z = g // 2
    n_z = n_graph // 2
    sibling = g + 1 - 2 * core
    width, nodes = feat_v.shape
    n_rows = adj.shape[0]
    row_blocks, blocks = n_rows // TILE, nodes // TILE
    hidden = hid.shape[0]
    share = CPAD // n_feat
    strip = width // n_dp
    pair = TPO * TILE
    part = width // PARTS
    own_rows = rows_at(x * width, width)

    barrier = pltpu.get_barrier_semaphore()

    def greet(d):
        pl.semaphore_signal(barrier, inc=1, device_id={"graph": lax.rem(g + d, n_graph)}, device_id_type=MESH)

    loop(1, n_graph, greet)
    for d in range(1, n_feat):
        pl.semaphore_signal(barrier, inc=1, device_id={"feat": lax.rem(x + d, n_feat)}, device_id_type=MESH)
    for d in range(1, n_dp):
        pl.semaphore_signal(barrier, inc=1, device_id={"dp": lax.rem(y + d, n_dp)}, device_id_type=MESH)

    load_bits = pltpu.make_async_copy(bits_h, bits, sem_local.at[0])
    load_bits.start()
    w1_src = (w1s_h, w1n_h)
    own_w1 = [
        pltpu.make_async_copy(w1_src[k].at[:, lanes(x * hidden, hidden)], w1f.at[k, own_rows, :], sem_local.at[1 + k])
        for k in range(2)
    ]
    for c in own_w1:
        c.start()
    featf[own_rows, :] = feat_v[...]
    for i in range(PARTS):
        for b in range(blocks):
            featb[i, b] = feat_v[i * part : (i + 1) * part, b * TILE : (b + 1) * TILE]
    cols_w[:, :, :n_graph] = cols_v[...]
    req_v[g] = cols_w[...]

    pl.semaphore_wait(barrier, n_graph - 1 + n_feat - 1 + n_dp - 1)

    def request(d):
        to = lax.rem(g + d, n_graph)
        return remote(cols_w, req_v.at[g], sem_req_s.at[d], sem_req_r.at[d], {"graph": to})

    loop(1, n_graph, lambda d: request(d).start())

    gather_feat = RingGather(featf, 0, width, width, sem_g_s.at[0], sem_g_r.at[0], x, n_feat)
    gather_q = RingGather(dq, CPAD, share, share, sem_g_s.at[1], sem_g_r.at[1], x, n_feat)
    gather_l = RingGather(lt, 0, share, share, sem_g_s.at[2], sem_g_r.at[2], x, n_feat)
    gather_ax = [
        RingGather(axf, i * part, width, part, sem_g_s.at[3 + i], sem_g_r.at[3 + i], x, n_feat) for i in range(PARTS)
    ]

    loop(1, n_graph, lambda d: request(d).wait_recv())
    fetch = pltpu.make_async_copy(req_v, req_s, sem_local.at[3])
    fetch.start()
    fetch.wait()

    def feats(i, d):
        to = lax.rem(g + d, n_graph)
        return remote(send.at[i, to], arr.at[i, g], sem_f_s.at[i, d], sem_f_r.at[i, d], {"graph": to})

    def pick(i, to, dst):
        for s in range(TPO):
            dst[i, to, :, s * TILE : (s + 1) * TILE] = featb[i, req_s[to, s, 0, g]]

    def post(i, k):
        d = spread_order(k, n_graph)
        to = lax.rem(g + d, n_graph)
        pick(i, to, send)
        feats(i, d).start()

    loop(1, n_graph, lambda k: post(0, k))
    gather_feat.start()
    for i in range(PARTS):
        pick(i, g, arr)

    def weights(d, k):
        to = lax.rem(x + d, n_feat)
        return remote(
            w1_src[k].at[:, lanes(to * hidden, hidden)],
            w1f.at[k, own_rows, :],
            sem_w_s.at[k, d],
            sem_w_r.at[k, d],
            {"feat": to},
        )

    for k in range(2):
        for d in range(1, n_feat):
            weights(d, k).start()

    load_bits.wait()

    def build(o):
        for s in range(TPO):
            t = o * TPO + s
            on = (s < count_s[o]).astype(I32)
            tile = (bits[t] * on).astype(F32)
            row = rows_s[s, 0, o]
            for r in range(row_blocks):
                here = (row == r).astype(F32)
                adj[r * TILE : (r + 1) * TILE, lanes(t * TILE, TILE)] = (tile * here).astype(BF16)

    loop(0, n_graph, build)
    deg[...] = jnp.zeros(deg.shape, F32)

    def degree(o):
        deg[...] += dot_nt(jnp.ones((8, pair), BF16), adj[:, lanes(o * pair, pair)])

    loop(0, n_graph, degree)
    deg[...] = 1.0 / jnp.maximum(deg[...], 1.0)

    eye_c = identity(CPAD, dl_v.shape[0])
    quarter = nodes // 4

    def pad_classes(i):
        here = lanes(i * quarter, quarter)
        dq[:CPAD, here] = dot(eye_c, dl_v[:, here]).astype(BF16)

    loop(0, 4, pad_classes)
    w2t[:CPAD, :] = dot(eye_c, w2s_v[...]).astype(BF16)
    w2t[CPAD:, :] = dot(eye_c, w2n_v[...]).astype(BF16)
    eye = identity(hidden, hidden)
    w2c[...] = dot_nt(eye, w2t[...]).astype(BF16)

    own_d = dq[rows_at(x * share, share), :n_rows].astype(F32) * deg[0:1, :]
    for r in range(row_blocks):
        dinv[r] = own_d[:, r * TILE : (r + 1) * TILE].astype(BF16)

    def terms(o):
        for s in range(TPO):
            t = o * TPO + s
            on = (s < count_s[o]).astype(I32)
            tile = (bits[t] * on).astype(F32).astype(BF16)
            qsend[o, s] = dot(dinv[rows_s[s, 0, o]], tile).astype(BF16)

    loop(0, n_graph, terms)
    qarr[g, :TPO] = qsend[g]

    def blank(o):
        qarr[o, TPO] = jnp.zeros((share, TILE), BF16)

    loop(0, n_graph, blank)

    gather_feat.middle()
    for c in own_w1:
        c.wait()
    for k in range(2):
        for d in range(1, n_feat):
            weights(d, k).wait_recv()
        w1t[k] = dot_nt(eye, w1f[k]).astype(BF16)

    def q_terms(d):
        to = lax.rem(g + d, n_graph)
        return remote(qsend.at[to], qarr.at[g, pl.ds(0, TPO)], sem_q_s.at[d], sem_q_r.at[d], {"graph": to})

    for i in range(PARTS):
        acc[...] = dot_nt(arr[i, g], adj[:, lanes(g * pair, pair)])

        def arrive(k, i=i):
            d = spread_order(k, n_graph)
            feats(i, d).wait_recv()
            if i < PARTS - 1:
                post(i + 1, k)
            o = lax.rem(g + n_graph - d, n_graph)
            acc[...] += dot_nt(arr[i, o], adj[:, lanes(o * pair, pair)])

        loop(1, n_graph // 2, arrive)
        if i > 0:
            gather_ax[i - 1].middle()
        if i == PARTS - 1:
            loop(1, n_graph, lambda d: q_terms(d).start())
        loop(n_graph // 2, n_graph, arrive)
        axf[rows_at(x * width + i * part, part), :] = (acc[...] * deg[0:1, :]).astype(BF16)
        gather_ax[i].start()
        if i == 0:
            gather_feat.arrive()

            def own_layer(n):
                here = lanes(n * quarter, quarter)
                pre[:, here] = dot(w1t[0], featf[:, here])

            loop(0, 4, own_layer)

    own_q = rows_at(CPAD + x * share, share)
    gather_ax[PARTS - 1].middle()
    loop(1, n_graph, lambda d: q_terms(d).wait_recv())

    def column(c):
        total = jnp.zeros((share, TILE), F32)
        for o in range(n_graph):
            which = jnp.where(
                req_s[o, 0, 0, g] == c, 0, jnp.where(req_s[o, 1, 0, g] == c, 1, jnp.where(req_s[o, 2, 0, g] == c, 2, TPO))
            )
            total = total + qarr[o, which].astype(F32)
        dq[own_q, lanes(c * TILE, TILE)] = total.astype(BF16)

    loop(0, blocks, column)
    gather_q.start()

    for i in range(PARTS):
        gather_ax[i].arrive()

    def layer(n, with_neighbours):
        here = lanes(n * quarter, quarter)
        v = pre[:, here]
        if with_neighbours:
            v = v + dot(w1t[1], axf[:, here])
        sig = 1.0 / (1.0 + jnp.exp(-v))
        act = (v * sig).astype(BF16)
        hid[:, here] = act
        pp[:, here] = dot(w2t[...], act).astype(BF16)
        pre[:, here] = sig * (1.0 + v * (1.0 - sig))

    loop(0, 3, lambda n: layer(n, True))
    layer(3, False)

    def scatter(d, k):
        to = lax.rem(x + d, n_feat)
        return remote(
            pp.at[rows_at(k * CPAD + to * share, share), :],
            pr.at[k, x],
            sem_p_s.at[k, d],
            sem_p_r.at[k, d],
            {"feat": to},
        )

    gather_q.middle()
    for d in range(1, n_feat):
        scatter(d, 1).start()

    gather_q.arrive()

    def backward(n):
        here = lanes(n * quarter, quarter)
        dpre[:, here] = (dot(w2c[...], dq[:, here]) * pre[:, here]).astype(BF16)

    loop(0, 4, backward)
    top = n_feat * strip

    def gradients(k):
        src, cols = ((featf, nodes), (axf, n_rows))[k]
        dp = dpre[:, :cols]

        t = dot_nt(src[...], dp)
        for o in range(n_feat):
            for i in range(n_dp):
                at = o * width + i * strip
                grad[k, i, o * strip : (o + 1) * strip, :] = t[at : at + strip]
        t = dot_nt(dq[k * CPAD : (k + 1) * CPAD, :], hid[...])
        for i in range(n_dp):
            grad[k, i, top:, :] = t[i * share : (i + 1) * share]

    gradients(0)
    gradients(1)
    core_send = remote(grad.at[1 - core], cr, sem_c_s, sem_c_r, {"graph": sibling})
    core_send.start()

    def score_sum(k, b):
        here = slice(b * TILE, (b + 1) * TILE)
        total = pr[k, 0, :, here].astype(F32)
        for o in range(1, n_feat):
            total = total + pr[k, o, :, here].astype(F32)
        return total

    for d in range(1, n_feat):
        scatter(d, 1).wait_recv()
    pr[1, x] = pp[rows_at(CPAD + x * share, share), :]
    pr[0, x] = pp[rows_at(x * share, share), :]
    for b in range(blocks):
        pb[b] = score_sum(1, b).astype(BF16)

    def scores(d):
        to = lax.rem(g + d, n_graph)
        return remote(psend.at[to], parr.at[g], sem_a_s.at[d], sem_a_r.at[d], {"graph": to})

    def pick_scores(to, dst):
        for s in range(TPO):
            dst[to, :, s * TILE : (s + 1) * TILE] = pb[req_s[to, s, 0, g]]

    def post_scores(k):
        d = spread_order(k, n_graph)
        to = lax.rem(g + d, n_graph)
        pick_scores(to, psend)
        scores(d).start()

    loop(1, n_graph, post_scores)
    pick_scores(g, parr)
    for d in range(1, n_feat):
        scatter(d, 0).start()

    core_send.wait_recv()
    for i in range(n_dp):
        total = grad[core, i] + cr[i]
        grad[core, i] = total
        ys[i] = total.astype(BF16)

    def over_y(d):
        to = lax.rem(y + d, n_dp)
        return remote(ys.at[to], yr.at[y], sem_y_s.at[d], sem_y_r.at[d], {"dp": to})

    for d in range(1, n_dp):
        over_y(d).start()

    for d in range(1, n_dp):
        over_y(d).wait_recv()
    total = grad[core, y]
    for d in range(1, n_dp):
        total = total + yr[lax.rem(y + d, n_dp)].astype(F32)
    xs[...] = total
    tz[top : top + share, :] = total[top:]
    tz[top + share :, :] = jnp.zeros((tz.shape[0] - top - share, hidden), F32)

    def over_x(d):
        to = lax.rem(x + d, n_feat)
        return remote(
            xs.at[rows_at(to * strip, strip), :],
            tz.at[rows_at(x * strip, strip), :],
            sem_x_s.at[d],
            sem_x_r.at[d],
            {"feat": to},
        )

    for d in range(1, n_feat):
        over_x(d).start()
    own_strip = rows_at(x * strip, strip)
    tz[own_strip, :] = xs[own_strip, :]
    for d in range(1, n_feat):
        over_x(d).wait_recv()

    piece = tz.shape[0] // n_z

    def over_z(d):
        to = lax.rem(z + d, n_z)
        return remote(
            tz.at[rows_at(to * piece, piece), :], zr.at[z], sem_z_s.at[d], sem_z_r.at[d], {"graph": to * 2 + core}
        )

    loop(1, n_z, lambda d: over_z(d).start())

    pacc[...] = dot_nt(parr[g], adj[:, lanes(g * pair, pair)])

    def arrive_scores(k):
        d = spread_order(n_graph - k, n_graph)
        scores(d).wait_recv()
        o = lax.rem(g + n_graph - d, n_graph)
        pacc[...] += dot_nt(parr[o], adj[:, lanes(o * pair, pair)])

    loop(1, n_graph, arrive_scores)
    for d in range(1, n_feat):
        scatter(d, 0).wait_recv()
    own_classes = rows_at(x * share, share)
    for b in range(blocks):
        here = slice(b * TILE, (b + 1) * TILE)
        total = score_sum(0, b)
        if b < row_blocks:
            total = total + pacc[:, here] * deg[0:1, here]
        lt[own_classes, here] = total.astype(BF16)
    gather_l.start()

    loop(1, n_z, lambda d: over_z(d).wait_recv())
    own_piece = rows_at(z * piece, piece)
    total = tz[own_piece, :]
    for d in range(1, n_z):
        total = total + zr[lax.rem(z + d, n_z)]
    held = tz.shape[0]

    def held_rows(owner):
        return (core * n_dp + owner) * held

    own_fin = rows_at(held_rows(y) + z * piece, piece)
    fin[own_fin, :] = total.astype(BF16)

    def spread_z(d):
        mine = fin.at[own_fin, :]
        return remote(mine, mine, sem_zg_s.at[d], sem_zg_r.at[d], {"graph": lax.rem(z + d, n_z) * 2 + core})

    loop(1, n_z, lambda d: spread_z(d).start())
    loop(1, n_z, lambda d: spread_z(d).wait_recv())
    gather_l.middle()

    gather_y = RingGather(fin, core * n_dp * held, held, held, sem_yg_s, sem_yg_r, y, n_dp, "dp")

    def spread_core(d):
        rows = fin.at[rows_at(held_rows(lax.rem(y + d, n_dp)), held), :]
        return remote(rows, rows, sem_cg_s.at[d], sem_cg_r.at[d], {"graph": sibling})

    gather_y.start()
    spread_core(0).start()
    gather_y.middle()
    spread_core(1).start()
    spread_core(n_dp - 1).start()
    gather_y.arrive()
    spread_core(2).start()
    gather_l.arrive()
    for d in range(n_dp):
        spread_core(d).wait_recv()

    for k in range(2):
        for i in range(n_dp):
            base = (k * n_dp + i) * held
            for o in range(n_feat):
                first_o[k, i * strip : (i + 1) * strip, o * hidden : (o + 1) * hidden] = fin[
                    base + o * strip : base + (o + 1) * strip, :
                ]
            second_o[k, i * share : (i + 1) * share, :] = fin[base + top : base + top + share, :]

    def settle(d):
        request(d).wait_send()
        q_terms(d).wait_send()
        scores(d).wait_send()
        for i in range(PARTS):
            feats(i, d).wait_send()

    loop(1, n_graph, settle)

    def settle_z(d):
        over_z(d).wait_send()
        spread_z(d).wait_send()

    loop(1, n_z, settle_z)
    core_send.wait_send()
    for d in range(1, n_feat):
        for k in range(2):
            weights(d, k).wait_send()
            scatter(d, k).wait_send()
        over_x(d).wait_send()
    for d in range(1, n_dp):
        over_y(d).wait_send()
    for d in range(n_dp):
        spread_core(d).wait_send()
    for ring in (gather_feat, gather_q, gather_l, gather_y, *gather_ax):
        ring.settle()


def fused_step(n_graph, n_feat, n_dp, rows, counts, cols, feat_t, dl_t, w2s_t, w2n_t, bits, w1s, w1n):
    width, nodes = feat_t.shape
    n_rows = nodes // 4 * 3
    n_slots, blocks = bits.shape[0], nodes // TILE
    hidden = w2s_t.shape[1]
    share = CPAD // n_feat
    strip = width // n_dp
    n_z = n_graph // 2
    held = n_feat * strip + share
    padded = -(-held // (16 * n_z)) * 16 * n_z
    part = width // PARTS
    pair = TPO * TILE
    vmem = pl.BlockSpec(memory_space=pltpu.VMEM)
    smem = pl.BlockSpec(memory_space=pltpu.SMEM)
    hbm = pl.BlockSpec(memory_space=pl.ANY)
    dma = pltpu.SemaphoreType.DMA
    return pl.pallas_call(
        functools.partial(step_kernel, n_graph, n_feat, n_dp),
        out_shape=(
            jax.ShapeDtypeStruct((CPAD, nodes), BF16),
            jax.ShapeDtypeStruct((2, width, n_feat * hidden), BF16),
            jax.ShapeDtypeStruct((2, CPAD, hidden), BF16),
        ),
        in_specs=[smem] * 2 + [vmem] * 5 + [hbm] * 3,
        out_specs=(vmem,) * 3,
        scratch_shapes=[
            pltpu.VMEM((2 * n_dp * padded, hidden), BF16),
            pltpu.VMEM((n_slots, TILE, TILE), I32),
            pltpu.VMEM((PARTS, blocks, part, TILE), BF16),
            pltpu.VMEM((n_feat * width, nodes), BF16),
            pltpu.VMEM((n_feat * width, n_rows), BF16),
            pltpu.VMEM((PARTS, n_graph, part, pair), BF16),
            pltpu.VMEM((PARTS, n_graph, part, pair), BF16),
            pltpu.VMEM((n_rows, n_slots * TILE), BF16),
            pltpu.VMEM((part, n_rows), F32),
            pltpu.VMEM((8, n_rows), F32),
            pltpu.VMEM((n_rows // TILE, share, TILE), BF16),
            pltpu.VMEM((n_graph, TPO, share, TILE), BF16),
            pltpu.VMEM((n_graph, TPO + 1, share, TILE), BF16),
            pltpu.VMEM((TPO, 1, TILE), I32),
            pltpu.VMEM((n_graph, TPO, 1, TILE), I32),
            pltpu.SMEM((n_graph, TPO, 1, TILE), I32),
            pltpu.VMEM((2, n_feat * width, hidden), BF16),
            pltpu.VMEM((2, hidden, n_feat * width), BF16),
            pltpu.VMEM((2 * CPAD, hidden), BF16),
            pltpu.VMEM((hidden, 2 * CPAD), BF16),
            pltpu.VMEM((2 * CPAD, nodes), BF16),
            pltpu.VMEM((hidden, nodes), F32),
            pltpu.VMEM((hidden, nodes), BF16),
            pltpu.VMEM((hidden, nodes), BF16),
            pltpu.VMEM((2 * CPAD, nodes), BF16),
            pltpu.VMEM((2, n_feat, share, nodes), BF16),
            pltpu.VMEM((blocks, share, TILE), BF16),
            pltpu.VMEM((n_graph, share, pair), BF16),
            pltpu.VMEM((n_graph, share, pair), BF16),
            pltpu.VMEM((share, n_rows), F32),
            pltpu.VMEM((2, n_dp, held, hidden), F32),
            pltpu.VMEM((n_dp, held, hidden), F32),
            pltpu.VMEM((n_dp, held, hidden), BF16),
            pltpu.VMEM((n_dp, held, hidden), BF16),
            pltpu.VMEM((held, hidden), F32),
            pltpu.VMEM((padded, hidden), F32),
            pltpu.VMEM((n_z, padded // n_z, hidden), F32),
            dma((4,)),
            dma((n_graph,)),
            dma((n_graph,)),
            dma((PARTS, n_graph)),
            dma((PARTS, n_graph)),
            dma((n_graph,)),
            dma((n_graph,)),
            dma((2, n_feat)),
            dma((2, n_feat)),
            dma((3 + PARTS, 4)),
            dma((3 + PARTS, 4)),
            dma((2, n_feat)),
            dma((2, n_feat)),
            dma((n_graph,)),
            dma((n_graph,)),
            dma,
            dma,
            dma((n_dp,)),
            dma((n_dp,)),
            dma((n_feat,)),
            dma((n_feat,)),
            dma((n_z,)),
            dma((n_z,)),
            dma((n_z,)),
            dma((n_z,)),
            dma((n_dp,)),
            dma((n_dp,)),
            dma((n_dp,)),
            dma((n_dp,)),
        ],
        compiler_params=pltpu.CompilerParams(
            collective_id=0, has_side_effects=True, vmem_limit_bytes=60 * 1024 * 1024
        ),
    )(rows, counts, cols, feat_t, dl_t, w2s_t, w2n_t, bits, w1s, w1n)


def on_device(
    n_graph,
    n_feat,
    n_dp,
    features,
    w1_self,
    w1_neigh,
    w2_self,
    w2_neigh,
    tile_rows,
    tile_cols,
    tile_count,
    tile_bits,
    d_logits,
):
    classes = d_logits.shape[2]
    lt, first, second = fused_step(
        n_graph,
        n_feat,
        n_dp,
        tile_rows[0, 0].T[:, None],
        tile_count[0, 0],
        tile_cols[0, 0].T[:, None],
        features[0].T,
        d_logits[0].T,
        w2_self.T,
        w2_neigh.T,
        tile_bits[0, 0].reshape(-1, TILE, TILE),
        w1_self,
        w1_neigh,
    )
    logits = lt[:classes].astype(F32).T
    first, second = first.astype(F32), second[:, :classes].astype(F32)
    return logits[None], first[0], first[1], second[0].T, second[1].T


def solution(mesh):
    placed = (
        P("dp", "graph", "feat"),
        P("feat", None),
        P("feat", None),
        P("feat", None),
        P("feat", None),
        P("dp", "graph", None, None),
        P("dp", "graph", None, None),
        P("dp", "graph", None),
        P("dp", "graph", None, None, None, None),
        P("dp", "graph", None),
    )
    return jax.shard_map(
        functools.partial(on_device, mesh.shape["graph"], mesh.shape["feat"], mesh.shape["dp"]),
        mesh=mesh,
        in_specs=placed,
        out_specs=(
            P("dp", "graph", None),
            P("feat", None),
            P("feat", None),
            P("feat", None),
            P("feat", None),
        ),
        check_vma=False,
    )
```

time: 565 us -> 159 us (0.28)
  waiting for transfers between devices: 400 us -> 0 us
  Pallas kernels: 0 us -> 149 us
  matrix products: 55.5 us -> 0 us
  local copies, waits for them, and re-layouts: 58.7 us -> 6.82 us
  starting transfers between devices: 26.1 us -> 0 us
  between operations: 14 us -> 0.68 us
  other arithmetic: 8.34 us -> 1.45 us
    psum x2 -> x0, waiting for transfers between devices: 232 us -> none  [the longest x1 190 us: on_device(): lax.psum((grad_first[0], grad_first[1], grad_second_self, grad_second_nei...]
    all_to_all x4 -> x0, waiting for transfers between devices: 168 us -> none  [the longest x2 92.8 us: gather_rows(): lax.all_to_all(picked, 'graph', split_axis=0, concat_axis=0, tiled=True)]
    pallas_call x0 -> x1, Pallas kernels: none -> 149 us  [fused_step(): pl.pallas_call(functools.partial(step_kernel, n_graph, n_feat, n_dp), out...]
    dot_general x16 -> x0, matrix products: 55.5 us -> none  [the longest x2 9.15 us: gather_rows(): jnp.dot(row_onehot, terms.reshape(n_slots, TILE * width), precision=highest)]
    all_to_all x4 -> x0, starting transfers between devices: 25.7 us -> none  [the longest x2 10.4 us: gather_rows(): lax.all_to_all(picked, 'graph', split_axis=0, concat_axis=0, tiled=True)]
    reshape x6 -> x0, local copies, waits for them, and re-layouts: 22.9 us -> none  [the longest x4 13.1 us: gather_rows(): return summed.reshape(node_count, width)]
    unnamed x41 -> x7, local copies, waits for them, and re-layouts: 21.8 us -> 3.7 us
    gather x3 -> x0, local copies, waits for them, and re-layouts: 7.62 us -> none  [the longest x2 5.04 us: gather_rows(): picked = source.reshape(block_count, TILE, width)[requested]]
  transfers between devices with their start and end apart: 8 -> 0, of which waited for: 6 -> 0; matrix products, arithmetic and copies ran while one was open for 14% -> 0% of each run, Pallas kernels for 0% -> 0%
where the time goes in v3:
time: 159 us; the launch traced here: 158 us
  Pallas kernels  149 us (94%)
  local copies, waits for them, and re-layouts  6.82 us (4%)
    pallas_call x1, Pallas kernels, fused_step(): pl.pallas_call(functools.partial(step_kernel, n_graph, n_feat, n_dp), out...  149 us
    unnamed x7, local copies, waits for them, and re-layouts  3.7 us

profile of v3, /device:TPU:1, one launch (start us, length us, event | category | flops | bytes accessed | tf_op | source)
XLA Modules:
  0.0 158.4 jit_solution(7269303916302322840)
XLA Ops:
  0.6 0.7 copy.23
  1.3 0.6 copy.15.rows_s
  1.9 0.7 copy.22
  2.6 0.6 copy.16.cols_v
  3.1 149.5 %shard_map.137 = (bf16[192,2048]{1,0:T(8,128)(2,1)}, bf16[2,192,1024]{2,1,0:T(8,128)(2,1)}, bf16[2,192,256]{2,1,0:T(8,128)(2,1)}) custom-call(s32[3,1,16]{2,1,0:T(1,128)} %copy.15.rows_s, s32[16]{0:T(128)} %bitcast.47, s32[3,1,16]{2,1,0:T(1,128)} %copy.16.cols_v, bf16[192,2048]{1,0:T(8,128)(2,1)} %bitcast.41, bf16[153,2048]{1,0:T(8,128)(2,1)} %bitcast.42, ...), custom_call_target="tpu_custom_call" | custom-call | tf_op jit(solution)/shard_map/pallas_call | solution.py:641
  152.6 1.3 convert_element_type.7
  153.9 0.0 copy-start.1
  153.9 0.0 copy-start
  153.9 1.2 slice_bitcast_fusion
  155.2 0.0 copy-done.1
  155.2 0.7 slice_bitcast_fusion.2
  156.0 0.0 copy-done
  156.0 0.1 convert_bitcast_fusion
  156.1 2.3 %copy.17 = f32[1,2048,153]{1,0,2:T(1,128)} copy(f32[1,2048,153]{1,2,0:T(8,128)S(1)} %convert_bitcast_fusion) | data formatting | bytes 2506752
  (1 shorter events, 0.0 us)
Async XLA Ops:
  153.9 1.3 copy-start.1
  153.9 2.0 %copy-start = (bf16[192,2048]{1,0:T(8,128)(2,1)S(1)}, bf16[192,2048]{1,0:T(8,128)(2,1)}, u32[]{:S(2)}) copy-start(bf16[192,2048]{1,0:T(8,128)(2,1)} %get-tuple-element.8) | copy-start | bytes 2359300
